TPU v7x, 256 devices: a whole 4x4x8 slice. The times are simulated.
256 devices in a mesh: row: 8 (over z), col: 32 (over x, y, core).
Axes of the slice: x: 4, y: 4, z: 8, core: 2. Of those that a mesh axis runs over, the one named last changes fastest.
Arguments:
- diag_tile: float32 [2048, 2048], P(('row', 'col')), as said below
- row_pan_u: float32 [8, 64, 2048], P('row', 'col'), may hold values from -6 to 6
- row_pan_v: float32 [8, 64, 2048], P('row', 'col'), may hold values from -0.5 to 0.5
- col_pan_u: float32 [32, 64, 2048], P('col', 'row'), may hold values from -6 to 6
- col_pan_v: float32 [32, 64, 2048], P('col', 'row'), may hold values from -0.5 to 0.5
- trail_u: float32 [8, 32, 64, 2048], P('row', 'col'), may hold values from -6 to 6
- trail_v: float32 [8, 32, 64, 2048], P('row', 'col'), may hold values from -6 to 6
Outputs:
- diag_factor: float32 [2048, 2048], P(('row', 'col'))
- row_solved: float32 [8, 64, 2048], P('row', 'col')
- col_solved: float32 [32, 64, 2048], P('col', 'row')
- grown_u: float32 [8, 32, 128, 2048], P('row', 'col')
- grown_v: float32 [8, 32, 128, 2048], P('row', 'col')
Inputs may be any that keep to these rules, and one draw needn't show every extreme that they name: `diag_tile`: symmetric positive definite: an exponential covariance of 2048 jittered sites on a grid, plus the identity.
All inputs are finite; a program needn't handle non-finite values.
Results may differ from a plain program's by a relative error of at most 0.0003.
Values sent between devices are 32-bit elements; how exact they have to be, the bound alone decides.
No kernel may reach another device: no remote copies, remote signals or barrier semaphores. Data moves between devices by JAX's collectives and lax.ppermute only.
A program may use at most 128 MiB of HBM per device.

v0:
```python
import jax
import jax.numpy as jnp
from jax import lax
from jax.sharding import PartitionSpec as P


def matmul(left, right):
    return jnp.dot(left, right, precision=lax.Precision.HIGHEST, preferred_element_type=jnp.float32)


def blocked_cholesky(matrix):
    size = matrix.shape[0]
    step = min(512, size)
    count = size // step
    working = matrix
    factor = jnp.zeros_like(matrix)
    inverses = []
    for block in range(count):
        start = block * step
        finish = start + step
        diag_block = jnp.linalg.cholesky(working[start:finish, start:finish])
        identity = jnp.eye(step, dtype=jnp.float32)
        block_inverse = lax.linalg.triangular_solve(
            diag_block, identity, left_side=True, lower=True
        )
        inverses.append(block_inverse)
        factor = factor.at[start:finish, start:finish].set(diag_block)
        if finish < size:
            below = matmul(working[finish:, start:finish], block_inverse.T)
            factor = factor.at[finish:, start:finish].set(below)
            working = working.at[finish:, finish:].add(-matmul(below, below.T))
    return (factor, inverses)


def solve_panel(factor, inverses, panel):
    count = panel.shape[0]
    width = panel.shape[1]
    length = panel.shape[2]
    step = inverses[0].shape[0]
    flat = panel.reshape(count * width, length)
    pieces = []
    for block in range(length // step):
        start = block * step
        finish = start + step
        residue = flat[:, start:finish]
        if block > 0:
            earlier = jnp.concatenate(pieces, axis=1)
            residue = residue - matmul(earlier, factor[start:finish, :start].T)
        pieces.append(matmul(residue, inverses[block].T))
    return jnp.concatenate(pieces, axis=1).reshape(count, width, length)


def body(diag_tile, row_pan_u, row_pan_v, col_pan_u, col_pan_v, trail_u, trail_v):
    gathered = lax.all_gather(diag_tile, ("row", "col"), axis=0, tiled=True)
    factor, inverses = blocked_cholesky(gathered)
    row_bases = lax.all_gather(row_pan_u, "col", axis=1, tiled=True)
    col_bases = lax.all_gather(col_pan_u, "row", axis=1, tiled=True)
    row_own = solve_panel(factor, inverses, row_pan_v)
    col_own = solve_panel(factor, inverses, col_pan_v)
    row_full = lax.all_gather(row_own, "col", axis=1, tiled=True)
    col_full = lax.all_gather(col_own, "row", axis=1, tiled=True)
    coupling = jnp.einsum("arx,bsx->abrs", row_full, col_full, precision=lax.Precision.HIGHEST)
    update = -jnp.einsum("abrs,arx->absx", coupling, row_bases, precision=lax.Precision.HIGHEST)
    grown_u = jnp.concatenate([trail_u, update], axis=2)
    spread = col_bases[None]
    grown_v = jnp.concatenate([trail_v, spread], axis=2)
    own_count = diag_tile.shape[0]
    factor_rows = lax.dynamic_slice_in_dim(
        factor, lax.axis_index(("row", "col")) * own_count, own_count, 0
    )
    return (factor_rows, row_own, col_own, grown_u, grown_v)


def solution(mesh):
    placed = (
        P(("row", "col"), None),
        P("row", "col", None),
        P("row", "col", None),
        P("col", "row", None),
        P("col", "row", None),
        P("row", "col", None, None),
        P("row", "col", None, None),
    )
    return jax.shard_map(
        body,
        mesh=mesh,
        in_specs=placed,
        out_specs=(
            P(("row", "col"), None),
            P("row", "col", None),
            P("col", "row", None),
            P("row", "col", None, None),
            P("row", "col", None, None),
        ),
        check_vma=False,
    )
```

profile of v0, /device:TPU:1, one launch (start us, length us, event | category | flops | bytes accessed | tf_op | source)
XLA Modules:
  0.0 934.4 jit_solution(17401307567017835977)
XLA Ops:
  8.7 28.6 %all_gather.18 = f32[1,64,2048]{2,0,1:T(1,128)} all-gather(f32[1,2,2048]{2,0,1:T(1,128)S(1)} %copy.31), channel_id=1, replica_groups=mesh['row'=8,'col'=32] {'col'}, dimensions={1}, use_global_device_ids=true | all-gather | bytes 540672 | tf_op jit(solution)/shard_map/all_gather | solution.py:56
  37.4 24.4 %all_gather.19 = f32[1,64,2048]{2,1,0:T(8,128)S(1)} all-gather(f32[1,8,2048]{2,1,0:T(8,128)} %param.33), channel_id=1, replica_groups=mesh['row'=8,'col'=32] {'row'}, dimensions={1}, use_global_device_ids=true | all-gather | bytes 589824 | tf_op jit(solution)/shard_map/all_gather | solution.py:57
  64.0 77.0 %all-gather.5.cloned.1.call-done = f32[2048,2048]{1,0:T(8,128)} async-done(((f32[8,2048]{1,0:T(8,128)}), f32[2048,2048]{1,0:T(8,128)}) %all-gather.5.cloned.1.call-update) | async-done | bytes 16777232 | tf_op jit(solution)/shard_map/all_gather | solution.py:54
  141.0 8.1 slice.500
  149.1 10.1 %copy.37 = f32[1536,1536]{0,1:T(8,128)} copy(f32[1536,1536]{1,0:T(8,128)} %slice.500) | data formatting | bytes 18874368
  162.3 11.7 %cholesky.462 = f32[128,128]{1,0:T(8,128)S(1)} custom-call(f32[128,128]{1,0:T(8,128)S(1)} %cholesky.746), custom_call_target="Cholesky" | custom-call | tf_op jit(solution)/shard_map/jit(cholesky)/cholesky | solution.py:21
  174.2 9.8 %custom-call.35 = f32[1,128,128]{1,2,0:T(8,128)S(1)} custom-call(f32[1,128,128]{2,1,0:T(8,128)S(1)} %get-tuple-element.246), custom_call_target="InvertDiagBlocksLowerTriangular" | custom-call | tf_op jit(solution)/shard_map/jit(cholesky)/cholesky | solution.py:21
  184.7 11.7 %cholesky.481 = f32[128,128]{1,0:T(8,128)S(1)} custom-call(f32[128,128]{1,0:T(8,128)S(1)} %cholesky.750), custom_call_target="Cholesky" | custom-call | tf_op jit(solution)/shard_map/jit(cholesky)/cholesky | solution.py:21
  196.5 10.0 %custom-call.36 = f32[1,128,128]{1,2,0:T(8,128)S(1)} custom-call(f32[1,128,128]{2,1,0:T(8,128)S(1)} %get-tuple-element.243), custom_call_target="InvertDiagBlocksLowerTriangular" | custom-call | tf_op jit(solution)/shard_map/jit(cholesky)/cholesky | solution.py:21
  207.1 11.7 %cholesky.502 = f32[128,128]{1,0:T(8,128)S(1)} custom-call(f32[128,128]{1,0:T(8,128)S(1)} %cholesky.755), custom_call_target="Cholesky" | custom-call | tf_op jit(solution)/shard_map/jit(cholesky)/cholesky | solution.py:21
  218.8 9.8 %custom-call.37 = f32[1,128,128]{1,2,0:T(8,128)S(1)} custom-call(f32[1,128,128]{2,1,0:T(8,128)S(1)} %get-tuple-element.240), custom_call_target="InvertDiagBlocksLowerTriangular" | custom-call | tf_op jit(solution)/shard_map/jit(cholesky)/cholesky | solution.py:21
  229.3 11.7 %cholesky.519 = f32[128,128]{1,0:T(8,128)S(1)} custom-call(f32[128,128]{1,0:T(8,128)S(1)} %convolution_subtract_fusion.23), custom_call_target="Cholesky" | custom-call | tf_op jit(solution)/shard_map/jit(cholesky)/cholesky | solution.py:21
  247.1 8.0 while.18
  255.1 39.3 %custom-call.38 = f32[4,128,128]{1,2,0:T(8,128)S(1)} custom-call(f32[4,128,128]{2,1,0:T(8,128)S(1)} %get-tuple-element.153), custom_call_target="InvertDiagBlocksLowerTriangular" | custom-call | tf_op jit(solution)/shard_map/triangular_solve/custom-call.3 | solution.py:23
  298.3 7.1 fusion
  307.8 20.2 %negate_add_fusion = f32[1536,1536]{0,1:T(8,128)S(1)} fusion(f32[1536,1536]{0,1:T(8,128)} %copy.37, f32[512,1536]{1,0:T(8,128)S(1)} %fusion), kind=kOutput, calls=%fused_computation.8 | convolution fusion | flops 14500233216 | bytes 22020096 | tf_op jit(solution)/shard_map/dot_general | solution.py:8
  333.5 11.7 %cholesky.534 = f32[128,128]{1,0:T(8,128)S(1)} custom-call(f32[128,128]{1,0:T(8,128)S(1)} %cholesky.759), custom_call_target="Cholesky" | custom-call | tf_op jit(solution)/shard_map/jit(cholesky)/cholesky | solution.py:21
  345.4 9.8 %custom-call.39 = f32[1,128,128]{1,2,0:T(8,128)S(1)} custom-call(f32[1,128,128]{2,1,0:T(8,128)S(1)} %get-tuple-element.236), custom_call_target="InvertDiagBlocksLowerTriangular" | custom-call | tf_op jit(solution)/shard_map/jit(cholesky)/cholesky | solution.py:21
  356.5 11.7 %cholesky.553 = f32[128,128]{1,0:T(8,128)S(1)} custom-call(f32[128,128]{1,0:T(8,128)S(1)} %cholesky.763), custom_call_target="Cholesky" | custom-call | tf_op jit(solution)/shard_map/jit(cholesky)/cholesky | solution.py:21
  368.3 10.2 %custom-call.40 = f32[1,128,128]{1,2,0:T(8,128)S(1)} custom-call(f32[1,128,128]{2,1,0:T(8,128)S(1)} %get-tuple-element.233), custom_call_target="InvertDiagBlocksLowerTriangular" | custom-call | tf_op jit(solution)/shard_map/jit(cholesky)/cholesky | solution.py:21
  380.7 13.2 %cholesky.574 = f32[128,128]{1,0:T(8,128)} custom-call(f32[128,128]{1,0:T(8,128)} %cholesky.768), custom_call_target="Cholesky" | custom-call | tf_op jit(solution)/shard_map/jit(cholesky)/cholesky | solution.py:21
  395.4 11.3 %custom-call.41 = f32[1,128,128]{1,2,0:T(8,128)} custom-call(f32[1,128,128]{2,1,0:T(8,128)} %get-tuple-element.230), custom_call_target="InvertDiagBlocksLowerTriangular" | custom-call | tf_op jit(solution)/shard_map/jit(cholesky)/cholesky | solution.py:21
  408.1 11.7 %cholesky.591 = f32[128,128]{1,0:T(8,128)S(1)} custom-call(f32[128,128]{1,0:T(8,128)S(1)} %convolution_subtract_fusion.22), custom_call_target="Cholesky" | custom-call | tf_op jit(solution)/shard_map/jit(cholesky)/cholesky | solution.py:21
  425.2 7.9 scatter.24
  438.4 8.0 while.19
  447.4 39.3 %custom-call.42 = f32[4,128,128]{1,2,0:T(8,128)S(1)} custom-call(f32[4,128,128]{2,1,0:T(8,128)S(1)} %get-tuple-element.154), custom_call_target="InvertDiagBlocksLowerTriangular" | custom-call | tf_op jit(solution)/shard_map/triangular_solve/custom-call.3 | solution.py:23
  492.7 9.8 %constant_dynamic-update-slice_fusion.17 = (f32[2048,2048]{1,0:T(8,128)}, f32[1024,512]{1,0:T(8,128)S(1)}) fusion(f32[2048,2048]{1,0:T(8,128)} %get-tuple-element.204, f32[128,512]{1,0:T(8,128)S(1)} %fusion.136, f32[128,512]{1,0:T(8,128)S(1)} %fusion.137, f32[128,512]{1,0:T(8,128)S(1)} %fusion.139, f32[128,512]{1,0:T(8,128)S(1)} %fusion.86, ...), kind=kOutput, calls=%fused_computation.316 | convolution fusion | flops 3222011904 | bytes 7340032 | tf_op jit(solution)/shard_map/dot_general | solution.py:8
  502.4 10.5 %slice_add_fusion = f32[1024,1024]{0,1:T(8,128)} fusion(f32[1536,1536]{0,1:T(8,128)} %copy-done, f32[1024,512]{1,0:T(8,128)S(1)} %get-tuple-element.254), kind=kOutput, calls=%fused_computation.9 | convolution fusion | flops 6444548096 | bytes 12582912 | tf_op jit(solution)/shard_map/dot_general | solution.py:8
  519.2 11.7 %cholesky.606 = f32[128,128]{1,0:T(8,128)S(1)} custom-call(f32[128,128]{1,0:T(8,128)S(1)} %cholesky.772), custom_call_target="Cholesky" | custom-call | tf_op jit(solution)/shard_map/jit(cholesky)/cholesky | solution.py:21
  531.1 9.8 %custom-call.43 = f32[1,128,128]{1,2,0:T(8,128)S(1)} custom-call(f32[1,128,128]{2,1,0:T(8,128)S(1)} %get-tuple-element.226), custom_call_target="InvertDiagBlocksLowerTriangular" | custom-call | tf_op jit(solution)/shard_map/jit(cholesky)/cholesky | solution.py:21
  543.4 11.7 %cholesky.625 = f32[128,128]{1,0:T(8,128)S(1)} custom-call(f32[128,128]{1,0:T(8,128)S(1)} %cholesky.776), custom_call_target="Cholesky" | custom-call | tf_op jit(solution)/shard_map/jit(cholesky)/cholesky | solution.py:21
  555.2 10.0 %custom-call.44 = f32[1,128,128]{1,2,0:T(8,128)S(1)} custom-call(f32[1,128,128]{2,1,0:T(8,128)S(1)} %get-tuple-element.223), custom_call_target="InvertDiagBlocksLowerTriangular" | custom-call | tf_op jit(solution)/shard_map/jit(cholesky)/cholesky | solution.py:21
  566.7 11.7 %cholesky.646 = f32[128,128]{1,0:T(8,128)S(1)} custom-call(f32[128,128]{1,0:T(8,128)S(1)} %cholesky.781), custom_call_target="Cholesky" | custom-call | tf_op jit(solution)/shard_map/jit(cholesky)/cholesky | solution.py:21
  578.5 9.8 %custom-call.45 = f32[1,128,128]{1,2,0:T(8,128)S(1)} custom-call(f32[1,128,128]{2,1,0:T(8,128)S(1)} %get-tuple-element.220), custom_call_target="InvertDiagBlocksLowerTriangular" | custom-call | tf_op jit(solution)/shard_map/jit(cholesky)/cholesky | solution.py:21
  589.7 11.7 %cholesky.663 = f32[128,128]{1,0:T(8,128)S(1)} custom-call(f32[128,128]{1,0:T(8,128)S(1)} %convolution_subtract_fusion.21), custom_call_target="Cholesky" | custom-call | tf_op jit(solution)/shard_map/jit(cholesky)/cholesky | solution.py:21
  608.6 11.6 %while.20 = (s32[]{:T(128)}, f32[512,512]{1,0:T(8,128)}, s32[4,2]{0,1:T(2,128)S(1)}, f32[4,128,128]{2,1,0:T(8,128)S(1)}, s32[]{:T(128)}) while((s32[]{:T(128)}, f32[512,512]{1,0:T(8,128)}, s32[4,2]{0,1:T(2,128)S(1)}, f32[4,128,128]{2,1,0:T(8,128)S(1)}, s32[]{:T(128)}) %tuple.159), condition=%wide.while_cond.10.clone.1, body=%wide.while_body.10.clone.1.sunk | while | flops 2 | bytes 131189 | solution.py:23
  620.2 39.3 %custom-call.46 = f32[4,128,128]{1,2,0:T(8,128)S(1)} custom-call(f32[4,128,128]{2,1,0:T(8,128)S(1)} %get-tuple-element.155), custom_call_target="InvertDiagBlocksLowerTriangular" | custom-call | tf_op jit(solution)/shard_map/triangular_solve/custom-call.3 | solution.py:23
  679.1 11.9 %cholesky.678 = f32[128,128]{1,0:T(8,128)S(1)} custom-call(f32[128,128]{1,0:T(8,128)S(1)} %cholesky.785), custom_call_target="Cholesky" | custom-call | tf_op jit(solution)/shard_map/jit(cholesky)/cholesky | solution.py:21
  691.1 9.8 %custom-call.47 = f32[1,128,128]{1,2,0:T(8,128)S(1)} custom-call(f32[1,128,128]{2,1,0:T(8,128)S(1)} %get-tuple-element.216), custom_call_target="InvertDiagBlocksLowerTriangular" | custom-call | tf_op jit(solution)/shard_map/jit(cholesky)/cholesky | solution.py:21
  704.1 11.7 %cholesky.697 = f32[128,128]{1,0:T(8,128)S(1)} custom-call(f32[128,128]{1,0:T(8,128)S(1)} %cholesky.789), custom_call_target="Cholesky" | custom-call | tf_op jit(solution)/shard_map/jit(cholesky)/cholesky | solution.py:21
  715.9 9.8 %custom-call.48 = f32[1,128,128]{1,2,0:T(8,128)S(1)} custom-call(f32[1,128,128]{2,1,0:T(8,128)S(1)} %get-tuple-element.213), custom_call_target="InvertDiagBlocksLowerTriangular" | custom-call | tf_op jit(solution)/shard_map/jit(cholesky)/cholesky | solution.py:21
  728.8 13.6 %cholesky.718 = f32[128,128]{1,0:T(8,128)} custom-call(f32[128,128]{1,0:T(8,128)} %cholesky.794), custom_call_target="Cholesky" | custom-call | tf_op jit(solution)/shard_map/jit(cholesky)/cholesky | solution.py:21
  743.9 11.3 %custom-call.49 = f32[1,128,128]{1,2,0:T(8,128)} custom-call(f32[1,128,128]{2,1,0:T(8,128)} %get-tuple-element.210), custom_call_target="InvertDiagBlocksLowerTriangular" | custom-call | tf_op jit(solution)/shard_map/jit(cholesky)/cholesky | solution.py:21
  757.4 11.7 %cholesky.735 = f32[128,128]{1,0:T(8,128)S(1)} custom-call(f32[128,128]{1,0:T(8,128)S(1)} %convolution_subtract_fusion.20), custom_call_target="Cholesky" | custom-call | tf_op jit(solution)/shard_map/jit(cholesky)/cholesky | solution.py:21
  793.9 11.6 %while.21 = (s32[]{:T(128)}, f32[512,512]{1,0:T(8,128)}, s32[4,2]{0,1:T(2,128)S(1)}, f32[4,128,128]{2,1,0:T(8,128)S(1)}, s32[]{:T(128)}) while((s32[]{:T(128)}, f32[512,512]{1,0:T(8,128)}, s32[4,2]{0,1:T(2,128)S(1)}, f32[4,128,128]{2,1,0:T(8,128)S(1)}, s32[]{:T(128)}) %tuple.160), condition=%wide.while_cond.10.clone.2, body=%wide.while_body.10.clone.2.sunk | while | flops 2 | bytes 131189 | solution.py:23
  805.5 39.9 %custom-call.50 = f32[4,128,128]{1,2,0:T(8,128)} custom-call(f32[4,128,128]{2,1,0:T(8,128)S(1)} %get-tuple-element.156), custom_call_target="InvertDiagBlocksLowerTriangular" | custom-call | tf_op jit(solution)/shard_map/triangular_solve/custom-call.3 | solution.py:23
  873.3 19.2 %all-gather = f32[64,2048]{1,0:T(8,128)S(1)} all-gather(f32[8,2048]{1,0:T(8,128)S(1)} %get-tuple-element.205), channel_id=2, replica_groups=mesh['row'=8,'col'=32] {'row'}, dimensions={0}, use_global_device_ids=true | all-gather | bytes 589824 | tf_op jit(solution)/shard_map/all_gather | solution.py:61
  892.5 31.0 %all-gather.2 = f32[32,2,2048]{2,1,0:T(2,128)S(1)} all-gather(f32[1,2,2048]{2,1,0:T(2,128)S(1)} %maximum_bitcast_fusion), channel_id=3, replica_groups=mesh['row'=8,'col'=32] {'col'}, dimensions={0}, use_global_device_ids=true | all-gather | bytes 540672 | tf_op jit(solution)/shard_map/all_gather | solution.py:60
  (248 shorter events, 183.6 us)
Async XLA Ops:
  7.2 133.8 %all-gather.5.cloned.1.call-start = ((), (), s32[]{:S(2)}) async-start(), calls=%async_computation | async-start | bytes 16842752 | tf_op jit(solution)/shard_map/all_gather | solution.py:54
  37.4 259.1 %copy-start.1 = (f32[512,512]{1,0:T(8,128)}, f32[512,512]{1,0:T(8,128)S(1)}, u32[]{:S(2)}) copy-start(f32[512,512]{1,0:T(8,128)S(1)} %fusion.36) | copy-start | bytes 3145732
  295.7 2.0 copy-start.4
  296.6 1.1 copy-start.11
  297.7 0.7 copy-start.17
  328.0 3.6 copy-start
  331.6 93.6 %copy-start.3 = (f32[512,512]{1,0:T(8,128)S(1)}, f32[512,512]{1,0:T(8,128)}, u32[]{:S(2)}) copy-start(f32[512,512]{1,0:T(8,128)} %get-tuple-element.190) | copy-start | bytes 3145732
  355.8 0.7 copy-start.20
  433.1 53.6 %copy-start.2 = (f32[512,512]{1,0:T(8,128)S(1)}, f32[512,512]{1,0:T(8,128)}, u32[]{:S(2)}) copy-start(f32[512,512]{1,0:T(8,128)} %copy-done.1) | copy-start | bytes 3145732
  446.4 1.0 copy-start.8
  490.6 22.4 %copy-start.13 = (f32[128,512]{1,0:T(8,128)}, f32[128,512]{1,0:T(8,128)S(1)}, u32[]{:S(2)}) copy-start(f32[128,512]{1,0:T(8,128)S(1)} %fusion.137) | copy-start | bytes 786436
  492.7 20.3 %copy-start.18 = (f32[128,512]{1,0:T(8,128)}, f32[128,512]{1,0:T(8,128)S(1)}, u32[]{:S(2)}) copy-start(f32[128,512]{1,0:T(8,128)S(1)} %fusion.136) | copy-start | bytes 786436
  518.2 1.0 copy-start.10
  659.5 4.0 copy-start.22
  661.6 10.6 %copy-start.6 = (f32[128,512]{1,0:T(8,128)}, f32[128,512]{1,0:T(8,128)S(1)}, u32[]{:S(2)}) copy-start(f32[128,512]{1,0:T(8,128)S(1)} %fusion.133) | copy-start | bytes 786436
  663.5 8.8 copy-start.15
  666.4 5.8 copy-start.19
  666.4 105.3 %copy-start.5 = (f32[128,512]{1,0:T(8,128)S(1)}, f32[128,512]{1,0:T(8,128)}, u32[]{:S(2)}) copy-start(f32[128,512]{1,0:T(8,128)} %copy-done.4) | copy-start | bytes 786436
  678.1 1.0 copy-start.9
  703.5 0.7 copy-start.21
  777.9 77.7 %copy-start.12 = (f32[128,512]{1,0:T(8,128)S(1)}, f32[128,512]{1,0:T(8,128)}, u32[]{:S(2)}) copy-start(f32[128,512]{1,0:T(8,128)} %copy-done.11) | copy-start | bytes 786436
  777.9 77.7 %copy-start.24 = (f32[1,8,2048]{2,1,0:T(8,128)S(1)}, f32[1,8,2048]{2,1,0:T(8,128)}, u32[]{:S(2)}) copy-start(f32[1,8,2048]{2,1,0:T(8,128)} %param.34) | copy-start | bytes 196612
  783.6 76.2 %copy-start.14 = (f32[128,512]{1,0:T(8,128)S(1)}, f32[128,512]{1,0:T(8,128)}, u32[]{:S(2)}) copy-start(f32[128,512]{1,0:T(8,128)} %copy-done.13) | copy-start | bytes 786436
  789.3 75.8 %copy-start.7 = (f32[128,512]{1,0:T(8,128)S(1)}, f32[128,512]{1,0:T(8,128)}, u32[]{:S(2)}) copy-start(f32[128,512]{1,0:T(8,128)} %copy-done.6) | copy-start | bytes 786436
  854.6 69.8 %copy-start.16 = (f32[1,64,2048]{2,0,1:T(1,128)S(1)}, f32[1,64,2048]{2,0,1:T(1,128)}, u32[]{:S(2)}) copy-start(f32[1,64,2048]{2,0,1:T(1,128)} %all_gather.18) | copy-start | bytes 1572868
  855.6 71.6 %copy-start.23 = (f32[1,2,2048]{2,1,0:T(2,128)}, f32[1,2,2048]{2,1,0:T(2,128)S(1)}, u32[]{:S(2)}) copy-start(f32[1,2,2048]{2,1,0:T(2,128)S(1)} %maximum_bitcast_fusion) | copy-start | bytes 49156
Sparse Core Ops, SparseCore 0:
  11.8 129.1 all-gather.4
where the time goes:
time: 940 us; the launch traced here: 934 us
  other arithmetic  500 us (53%)
  matrix products  135 us (14%)
  blocking collectives  103 us (11%)
  local copies, waits for them, and re-layouts  91.5 us (10%)
  waiting for transfers between devices  77.7 us (8%)
  between operations  26.3 us (3%)
    another operation x59, other arithmetic, blocked_cholesky(): diag_block = jnp.linalg.cholesky(working[start:finish, start:finish])  325 us
    another operation x9, other arithmetic, blocked_cholesky(): lax.linalg.triangular_solve(diag_block, identity, left_side=True, lower=T...  164 us
    dot_general x20, matrix products, matmul(): jnp.dot(left, right, precision=lax.Precision.HIGHEST, preferred_element_t...  90.8 us
    all_gather x1, waiting for transfers between devices, body(): gathered = lax.all_gather(diag_tile, ('row', 'col'), axis=0, tiled=True)  77 us
    another operation x53, local copies, waits for them, and re-layouts, blocked_cholesky(): lax.linalg.triangular_solve(diag_block, identity, left_side=True, lower=T...  38.9 us
    all_gather x1, blocking collectives, body(): row_full = lax.all_gather(row_own, 'col', axis=1, tiled=True)  31 us
    all_gather x1, blocking collectives, body(): row_bases = lax.all_gather(row_pan_u, 'col', axis=1, tiled=True)  28.6 us
    another operation x28, matrix products, blocked_cholesky(): lax.linalg.triangular_solve(diag_block, identity, left_side=True, lower=T...  24.9 us
  transfers between devices with their start and end apart: 1, of which 1 were waited for; matrix products, arithmetic and copies ran while one was open for 0% of the time, Pallas kernels for 0%

commit v1 on v0

v1 whole, which is shorter than its diff:
```python
import jax
import jax.numpy as jnp
from jax import lax
from jax.experimental import pallas as pl
from jax.experimental.pallas import tpu as pltpu
from jax.sharding import PartitionSpec as P

F32 = jnp.float32
BF16 = jnp.bfloat16
SIZE = 2048
PANEL = 256
COUNT = SIZE // PANEL
HALF = PANEL // 2
RANK = 64
NT = (((1,), (1,)), ((), ()))
TN = (((0,), (0,)), ((), ()))
NN = (((1,), (0,)), ((), ()))


def exact(left, right, dims):
    return lax.dot_general(left, right, dims, precision=lax.Precision.HIGHEST, preferred_element_type=F32)


def split(value):
    high = value.astype(BF16)
    return high, (value - high.astype(F32)).astype(BF16)


def iota(shape, dim):
    return lax.broadcasted_iota(jnp.int32, shape, dim)


def along_rows(value, row):
    return jnp.broadcast_to(value[row : row + 1, :], value.shape)


def along_lanes(value, lane):
    return jnp.broadcast_to(value[:, lane : lane + 1], value.shape)


def total(terms):
    while len(terms) > 1:
        terms = [
            terms[i] + terms[i + 1] if i + 1 < len(terms) else terms[i]
            for i in range(0, len(terms), 2)
        ]
    return terms[0]


def factor_block(block, groups=2):
    count = len(block)
    size = 8 * count
    width = 8 * groups
    work = list(block)
    sub = iota((8, size), 0)
    lane = iota((8, size), 1)
    side = [jnp.where(sub + 8 * i == lane, 1.0, 0.0).astype(F32) for i in range(count)]
    upper = [None] * count
    inverse = [None] * count
    for top in range(0, count, groups):
        rows = work[top : top + groups]
        eyes = side[top : top + groups]
        cols = [[along_lanes(rows[a], 8 * top + k) for a in range(groups)] for k in range(width)]
        below = {
            i: [along_lanes(work[i], 8 * top + k) for k in range(width)]
            for i in range(top + groups, count)
        }
        up = [jnp.zeros((8, size), F32)] * groups
        inv = [jnp.zeros((8, size), F32)] * groups
        for k in range(width):
            ka, ks = divmod(k, 8)
            pivot = along_rows(cols[k][ka], ks)
            scale = 1.0 / pivot
            root = lax.rsqrt(pivot)
            row_k = along_rows(rows[ka], ks)
            eye_k = along_rows(eyes[ka], ks)
            here = sub == ks
            up[ka] = jnp.where(here, row_k * root, up[ka])
            inv[ka] = jnp.where(here, eye_k * root, inv[ka])
            times = []
            for a in range(groups):
                ratio = cols[k][a] * scale
                times.append(jnp.where(here, 1.0 - scale, ratio) if a == ka else ratio)
            for a in range(groups):
                rows[a] = rows[a] - times[a] * row_k
                eyes[a] = eyes[a] - times[a] * eye_k
            for m in range(k + 1, width):
                col_m = along_rows(cols[m][ka], ks)
                cols[m] = [cols[m][a] - times[a] * col_m for a in range(groups)]
        upper[top : top + groups] = up
        inverse[top : top + groups] = inv
        row_all = [along_rows(rows[k // 8], k % 8) for k in range(width)]
        eye_all = [along_rows(eyes[k // 8], k % 8) for k in range(width)]
        for i in range(top + groups, count):
            work[i] = work[i] - total([below[i][k] * row_all[k] for k in range(width)])
            side[i] = side[i] - total([below[i][k] * eye_all[k] for k in range(width)])
    upper = [jnp.where(sub + 8 * i <= lane, upper[i], 0.0) for i in range(count)]
    inverse = [jnp.where(sub + 8 * i >= lane, inverse[i], 0.0) for i in range(count)]
    return jnp.concatenate(upper, axis=0), jnp.concatenate(inverse, axis=0)


def factor_values(value):
    return factor_block([value[8 * i : 8 * i + 8, :] for i in range(value.shape[0] // 8)])


def panel_kernel(
    place_ref, diag_ref, pan_ref, base_ref, trail_ref,
    own_ref, solved_ref, grown_ref,
    work, high, low, inverse, sems,
):
    own_tile = place_ref[0]
    own_row = pl.multiple_of(place_ref[1], 8)

    def fetch(k, slot):
        cols = pl.ds(pl.multiple_of(k * PANEL, PANEL), PANEL)
        return (
            pltpu.make_async_copy(diag_ref.at[:, cols], work.at[slot, pl.ds(0, SIZE)], sems.at[slot, 0]),
            pltpu.make_async_copy(pan_ref.at[:, cols], work.at[slot, pl.ds(SIZE, 2 * RANK)], sems.at[slot, 1]),
        )

    for copy in fetch(0, 0):
        copy.start()
    work[0, SIZE + 2 * RANK :, :] = jnp.zeros((PANEL - 2 * RANK, PANEL), F32)
    work[1, SIZE + 2 * RANK :, :] = jnp.zeros((PANEL - 2 * RANK, PANEL), F32)

    def step(k, carry):
        slot = lax.rem(k, 2)
        for copy in fetch(k, slot):
            copy.wait()

        @pl.when(k + 1 < COUNT)
        def _():
            for copy in fetch(k + 1, 1 - slot):
                copy.start()

        def rows_of(i):
            return pl.ds(pl.multiple_of(i * PANEL, PANEL), PANEL)

        def update(i, carry):
            def add(m, acc):
                left_high = high[m, rows_of(i), :]
                left_low = low[m, rows_of(i), :]
                right_high = high[m, rows_of(k), :]
                right_low = low[m, rows_of(k), :]
                dot = lambda a, b: lax.dot_general(a, b, NT, preferred_element_type=F32)
                return acc - (dot(left_high, right_high) + dot(left_high, right_low) + dot(left_low, right_high))

            work[slot, rows_of(i), :] = lax.fori_loop(0, k, add, work[slot, rows_of(i), :])
            return carry

        @pl.when(k > 0)
        def _():
            lax.fori_loop(k, COUNT + 1, update, 0)

        tile = work.at[slot, rows_of(k)]
        first_up, first_inv = factor_values(tile[:HALF, :HALF])
        cross = exact(tile[HALF:, :HALF], first_inv, NT)
        rest = tile[HALF:, HALF:] - exact(cross, cross, NT)
        second_up, second_inv = factor_values(rest)
        corner = -exact(second_inv, exact(cross, first_inv, NN), NN)
        zero = jnp.zeros((HALF, HALF), F32)
        inverse[:HALF, :HALF] = first_inv
        inverse[:HALF, HALF:] = zero
        inverse[HALF:, :HALF] = corner
        inverse[HALF:, HALF:] = second_inv
        tile[:HALF, :HALF] = first_up.T
        tile[:HALF, HALF:] = zero
        tile[HALF:, :HALF] = cross
        tile[HALF:, HALF:] = second_up.T

        def solve(i, carry):
            value = exact(work[slot, rows_of(i), :], inverse[...], NT)
            work[slot, rows_of(i), :] = value
            top, bottom = split(value)
            high[k, rows_of(i), :] = top
            low[k, rows_of(i), :] = bottom
            return carry

        lax.fori_loop(k + 1, COUNT + 1, solve, 0)
        cols = pl.ds(pl.multiple_of(k * PANEL, PANEL), PANEL)
        start = pl.multiple_of(own_tile * PANEL + own_row, 8)
        mine = work[slot, pl.ds(start, 8), :]
        own_ref[:, cols] = jnp.where(own_tile >= k, mine, 0.0)
        solved_ref[:, cols] = work[slot, SIZE : SIZE + 2 * RANK, :]
        return carry

    lax.fori_loop(0, COUNT, step, 0)
    coupling = exact(solved_ref[:RANK, :], solved_ref[RANK:, :], NT)
    grown_ref[:RANK, :] = trail_ref[...]
    grown_ref[RANK:, :] = -exact(coupling, base_ref[...], TN)


def panel_step(place, diag, pan, base, trail):
    vmem = pl.BlockSpec(memory_space=pltpu.VMEM)
    anywhere = pl.BlockSpec(memory_space=pl.ANY)
    return pl.pallas_call(
        panel_kernel,
        out_shape=(
            jax.ShapeDtypeStruct((8, SIZE), F32),
            jax.ShapeDtypeStruct((2 * RANK, SIZE), F32),
            jax.ShapeDtypeStruct((2 * RANK, SIZE), F32),
        ),
        in_specs=[pl.BlockSpec(memory_space=pltpu.SMEM), anywhere, anywhere, vmem, vmem],
        out_specs=(vmem, vmem, vmem),
        scratch_shapes=[
            pltpu.VMEM((2, SIZE + PANEL, PANEL), F32),
            pltpu.VMEM((COUNT, SIZE + PANEL, PANEL), BF16),
            pltpu.VMEM((COUNT, SIZE + PANEL, PANEL), BF16),
            pltpu.VMEM((PANEL, PANEL), F32),
            pltpu.SemaphoreType.DMA((2, 2)),
        ],
        compiler_params=pltpu.CompilerParams(vmem_limit_bytes=56 * 1024 * 1024),
    )(place, diag, pan, base, trail)


def body(diag_tile, row_pan_u, row_pan_v, col_pan_u, col_pan_v, trail_u, trail_v):
    row = lax.axis_index("row")
    col = lax.axis_index("col")
    diag = lax.all_gather(diag_tile, ("row", "col"), axis=0, tiled=True)
    row_all = lax.all_gather(jnp.stack([row_pan_u[0], row_pan_v[0]]), "col", axis=1, tiled=True)
    col_all = lax.all_gather(jnp.stack([col_pan_u[0], col_pan_v[0]]), "row", axis=1, tiled=True)
    pan = jnp.concatenate([row_all[1], col_all[1]], axis=0)
    place = jnp.stack([row, col * 8]).astype(jnp.int32)
    own, solved, grown_u = panel_step(place, diag, pan, row_all[0], trail_u[0, 0])
    row_own = lax.dynamic_slice_in_dim(solved, col * 2, 2, 0)
    col_own = lax.dynamic_slice_in_dim(solved, RANK + row * 8, 8, 0)
    grown_v = jnp.concatenate([trail_v[0, 0], col_all[0]], axis=0)
    return (own, row_own[None], col_own[None], grown_u[None, None], grown_v[None, None])


def solution(mesh):
    placed = (
        P(("row", "col"), None),
        P("row", "col", None),
        P("row", "col", None),
        P("col", "row", None),
        P("col", "row", None),
        P("row", "col", None, None),
        P("row", "col", None, None),
    )
    return jax.shard_map(
        body,
        mesh=mesh,
        in_specs=placed,
        out_specs=(
            P(("row", "col"), None),
            P("row", "col", None),
            P("col", "row", None),
            P("row", "col", None, None),
            P("row", "col", None, None),
        ),
        check_vma=False,
    )
```

time: 940 us -> 367 us (0.39)
  other arithmetic: 500 us -> 5.98 us
  matrix products: 135 us -> 0 us
  waiting for transfers between devices: 77.7 us -> 211 us
  Pallas kernels: 0 us -> 126 us
  blocking collectives: 103 us -> 0 us
  local copies, waits for them, and re-layouts: 91.5 us -> 9.42 us
  between operations: 26.3 us -> 13.8 us
    another operation x68 -> x3, other arithmetic: 489 us -> 2.84 us  [the longest x1 1.54 us: body(): jnp.stack([col_pan_u[0], col_pan_v[0]])]
    all_gather x1 -> x3, waiting for transfers between devices: 77 us -> 210 us  [the longest x1 123 us: body(): diag = lax.all_gather(diag_tile, ('row', 'col'), axis=0, tiled=True)]
    pallas_call x0 -> x1, Pallas kernels: none -> 126 us  [panel_step(): pl.pallas_call(panel_kernel, out_shape=(jax.ShapeDtypeStruct((8, SIZE), F...]
    all_gather x4 -> x0, blocking collectives: 103 us -> none  [the longest x1 31 us: body(): row_full = lax.all_gather(row_own, 'col', axis=1, tiled=True)]
    dot_general x22 -> x0, matrix products: 92.1 us -> none  [the longest x20 90.8 us: matmul(): jnp.dot(left, right, precision=lax.Precision.HIGHEST, preferred_element_t...]
    another operation x70 -> x0, local copies, waits for them, and re-layouts: 48.8 us -> none  [the longest x53 38.9 us: blocked_cholesky(): lax.linalg.triangular_solve(diag_block, identity, left_side=True, lower=T...]
    another operation x52 -> x0, matrix products: 43.1 us -> none  [the longest x28 24.9 us: blocked_cholesky(): lax.linalg.triangular_solve(diag_block, identity, left_side=True, lower=T...]
    unnamed x54 -> x4, local copies, waits for them, and re-layouts: 20.2 us -> 2.59 us
  transfers between devices with their start and end apart: 1 -> 3, of which waited for: 1 -> 3; matrix products, arithmetic and copies ran while one was open for 0% -> 3% of each run, Pallas kernels for 0% -> 0%
where the time goes in v1:
time: 367 us; the launch traced here: 366 us
  waiting for transfers between devices  211 us (57%)
  Pallas kernels  126 us (34%)
  between operations  13.8 us (4%)
  local copies, waits for them, and re-layouts  9.42 us (3%)
  other arithmetic  5.98 us (2%)
    pallas_call x1, Pallas kernels, panel_step(): pl.pallas_call(panel_kernel, out_shape=(jax.ShapeDtypeStruct((8, SIZE), F...  126 us
    all_gather x1, waiting for transfers between devices, body(): diag = lax.all_gather(diag_tile, ('row', 'col'), axis=0, tiled=True)  123 us
    all_gather x1, waiting for transfers between devices, body(): lax.all_gather(jnp.stack([row_pan_u[0], row_pan_v[0]]), 'col', axis=1, ti...  51.4 us
    all_gather x1, waiting for transfers between devices, body(): lax.all_gather(jnp.stack([col_pan_u[0], col_pan_v[0]]), 'row', axis=1, ti...  35.5 us
  transfers between devices with their start and end apart: 3, of which 3 were waited for; matrix products, arithmetic and copies ran while one was open for 3% of the time, Pallas kernels for 0%

profile of v1, /device:TPU:1, one launch (start us, length us, event | category | flops | bytes accessed | tf_op | source)
XLA Modules:
  0.0 366.2 jit_solution(18120540147631957062)
XLA Ops:
  7.2 0.0 all-gather.8.cloned.1.call-start
  7.2 1.5 pad_maximum_fusion.1
  8.7 0.0 all-gather.8.cloned.1.call-update
  8.8 0.0 all-gather.6.cloned.1.call-start
  8.8 0.7 copy.12
  9.6 0.7 copy.13
  10.3 0.6 pad_maximum_fusion.2
  11.0 0.0 all-gather.6.cloned.1.call-update
  11.0 0.0 all-gather.4.cloned.1.call-start
  11.0 0.7 all-gather.4.cloned.1.call-update
  11.7 0.7 pad_add_fusion.place_ref
  12.4 35.5 %all-gather.8.cloned.1.call-done = f32[2,64,2048]{2,1,0:T(8,128)} async-done(((f32[2,8,2048]{2,1,0:T(8,128)}), f32[2,64,2048]{2,1,0:T(8,128)}) %all-gather.8.cloned.1.call-update) | async-done | bytes 1048592 | tf_op jit(solution)/shard_map/all_gather | solution.py:221
  47.8 1.3 slice_bitcast_fusion
  49.1 2.1 maximum_bitcast_fusion
  51.2 51.4 %all-gather.6.cloned.1.call-done = f32[2,64,2048]{2,0,1:T(2,128)} async-done(((f32[2,2,2048]{2,0,1:T(2,128)}), f32[2,64,2048]{2,0,1:T(2,128)}) %all-gather.6.cloned.1.call-update) | async-done | bytes 1048592 | tf_op jit(solution)/shard_map/all_gather | solution.py:220
  102.6 2.6 fusion
  105.3 0.2 copy.21
  105.4 1.0 copy.20
  106.4 1.1 pad_maximum_fusion.pan_ref
  107.4 123.3 %all-gather.4.cloned.1.call-done.diag_ref = f32[2048,2048]{1,0:T(8,128)} async-done(((f32[8,2048]{1,0:T(8,128)}), f32[2048,2048]{1,0:T(8,128)}) %all-gather.4.cloned.1.call-update) | async-done | bytes 16777232 | tf_op jit(solution)/shard_map/all_gather | solution.py:219
  230.8 126.0 %shard_map.110 = (f32[8,2048]{1,0:T(8,128)}, f32[128,2048]{1,0:T(8,128)}, f32[128,2048]{1,0:T(8,128)}) custom-call(s32[2]{0:T(128)} %pad_add_fusion.place_ref, f32[2048,2048]{1,0:T(8,128)} %all-gather.4.cloned.1.call-done.diag_ref, f32[128,2048]{1,0:T(8,128)} %pad_maximum_fusion.pan_ref, f32[64,2048]{1,0:T(8,128)} %bitcast.21, f32[64,2048]{1,0:T(8,128)} %bitcast.23), custom_call_target="tpu_custom_call" | custom-call | tf_op jit(solution)/shard_map/pallas_call | solution.py:196
  356.7 1.5 dynamic-slice_bitcast_fusion.1
  358.2 1.5 dynamic-slice_bitcast_fusion
Async XLA Ops:
  7.2 40.7 %all-gather.8.cloned.1.call-start = ((), (), s32[]{:S(2)}) async-start(), calls=%async_computation.2 | async-start | bytes 1179648 | tf_op jit(solution)/shard_map/all_gather | solution.py:221
  8.8 93.9 %all-gather.6.cloned.1.call-start = ((), (), s32[]{:S(2)}) async-start(), calls=%async_computation.1 | async-start | bytes 1081344 | tf_op jit(solution)/shard_map/all_gather | solution.py:220
  11.0 219.8 %all-gather.4.cloned.1.call-start = ((), (), s32[]{:S(2)}) async-start(), calls=%async_computation | async-start | bytes 16842752 | tf_op jit(solution)/shard_map/all_gather | solution.py:219
Sparse Core Ops, SparseCore 0:
  10.4 37.4 all-gather.7
  51.0 51.6 all-gather.5
  106.5 124.2 all-gather.3

commit v2 on v1

v2 whole, which is shorter than its diff:
```python
import jax
import jax.numpy as jnp
import numpy as np
from jax import lax
from jax.experimental import pallas as pl
from jax.experimental.pallas import tpu as pltpu
from jax.sharding import PartitionSpec as P

F32 = jnp.float32
BF16 = jnp.bfloat16
SIZE = 2048
PANEL = 256
COUNT = SIZE // PANEL
HALF = PANEL // 2
RANK = 64
NT = (((1,), (1,)), ((), ()))
TN = (((0,), (0,)), ((), ()))
NN = (((1,), (0,)), ((), ()))
EARLY = 2
LANES = COUNT * 4


def tile_start(k, first):
    return sum(COUNT - j for j in range(first, k))


def exact(left, right, dims):
    return lax.dot_general(left, right, dims, precision=lax.Precision.HIGHEST, preferred_element_type=F32)


def split(value):
    high = value.astype(BF16)
    return high, (value - high.astype(F32)).astype(BF16)


def iota(shape, dim):
    return lax.broadcasted_iota(jnp.int32, shape, dim)


def along_rows(value, row):
    return jnp.broadcast_to(value[row : row + 1, :], value.shape)


def along_lanes(value, lane):
    return jnp.broadcast_to(value[:, lane : lane + 1], value.shape)


def total(terms):
    while len(terms) > 1:
        terms = [
            terms[i] + terms[i + 1] if i + 1 < len(terms) else terms[i]
            for i in range(0, len(terms), 2)
        ]
    return terms[0]


def factor_block(block, beside, groups=2):
    count = len(block)
    size = 8 * count
    width = 8 * groups
    work = list(block)
    sub = iota((8, size), 0)
    lane = iota((8, size), 1)
    side = [jnp.where(sub + 8 * i == lane, 1.0, 0.0).astype(F32) for i in range(count)]
    upper = [None] * count
    inverse = [None] * count
    for top in range(0, count, groups):
        beside(top // groups)
        rows = work[top : top + groups]
        eyes = side[top : top + groups]
        cols = [[along_lanes(rows[a], 8 * top + k) for a in range(groups)] for k in range(width)]
        below = {
            i: [along_lanes(work[i], 8 * top + k) for k in range(width)]
            for i in range(top + groups, count)
        }
        up = [jnp.zeros((8, size), F32)] * groups
        inv = [jnp.zeros((8, size), F32)] * groups
        for k in range(width):
            ka, ks = divmod(k, 8)
            pivot = along_rows(cols[k][ka], ks)
            scale = 1.0 / pivot
            root = lax.rsqrt(pivot)
            row_k = along_rows(rows[ka], ks)
            eye_k = along_rows(eyes[ka], ks)
            here = sub == ks
            up[ka] = jnp.where(here, row_k * root, up[ka])
            inv[ka] = jnp.where(here, eye_k * root, inv[ka])
            times = []
            for a in range(groups):
                ratio = cols[k][a] * scale
                times.append(jnp.where(here, 1.0 - scale, ratio) if a == ka else ratio)
            for a in range(groups):
                rows[a] = rows[a] - times[a] * row_k
                eyes[a] = eyes[a] - times[a] * eye_k
            for m in range(k + 1, width):
                col_m = along_rows(cols[m][ka], ks)
                cols[m] = [cols[m][a] - times[a] * col_m for a in range(groups)]
        upper[top : top + groups] = up
        inverse[top : top + groups] = inv
        row_all = [along_rows(rows[k // 8], k % 8) for k in range(width)]
        eye_all = [along_rows(eyes[k // 8], k % 8) for k in range(width)]
        for i in range(top + groups, count):
            work[i] = work[i] - total([below[i][k] * row_all[k] for k in range(width)])
            side[i] = side[i] - total([below[i][k] * eye_all[k] for k in range(width)])
    upper = [jnp.where(sub + 8 * i <= lane, upper[i], 0.0) for i in range(count)]
    inverse = [jnp.where(sub + 8 * i >= lane, inverse[i], 0.0) for i in range(count)]
    return jnp.concatenate(upper, axis=0), jnp.concatenate(inverse, axis=0)


def factor_values(value, beside):
    return factor_block([value[8 * i : 8 * i + 8, :] for i in range(value.shape[0] // 8)], beside)


def dot3(left_high, left_low, right_high, right_low):
    left = jnp.concatenate([left_high, left_low, left_high], axis=1)
    right = jnp.concatenate([right_high, right_high, right_low], axis=1)
    return lax.dot_general(left, right, NT, preferred_element_type=F32)


def start_fetch(place_ref, mine_ref, other_ref, work, sems, first, last):
    x0, y0, core = place_ref[2], place_ref[3], place_ref[4]
    for k in range(first, last):
        at = tile_start(k, first)
        for source, owner in ((mine_ref, core), (other_ref, 1 - core)):
            for outer in range(4):
                for inner in range(4):
                    dx = jnp.where(owner == 0, outer, inner)
                    dy = jnp.where(owner == 0, inner, outer)
                    group = (lax.rem(x0 - dx + 4, 4) * 4 + lax.rem(y0 - dy + 4, 4)) * 2 + owner
                    pltpu.make_async_copy(
                        source.at[outer, inner, pl.ds(at, COUNT - k)],
                        work.at[k - first, pl.ds(k, COUNT - k), group],
                        sems.at[k - first],
                    ).start()


def wait_fetch(k, work, sems, first, last):
    for j in range(first, last):

        @pl.when(k == j)
        def _():
            whole = work.at[j - first, pl.ds(j, COUNT - j)]
            pltpu.make_async_copy(whole, whole, sems.at[j - first]).wait()


SOLVES = 6
UPDATES = 26


def plan(first, last, rows):
    spare = last - first
    table = []
    for k in range(first, last):
        solves, updates = [], []
        if k > first:
            solves = [(k - 1 - first, i, k - 1) for i in range(k + 1, rows)]
        for m in range(k if k == first else k - 1, -1, -1) if k == first else [k - 1]:
            if m < k:
                updates += [(k - first, k, i, m) for i in range(k + 1, rows)]
        if k + 1 < last:
            updates += [(k + 1 - first, k + 1, i, m) for i in range(k + 1, rows) for m in range(k)]
        assert len(solves) <= SOLVES and len(updates) <= UPDATES
        solves += [(spare, 0, COUNT)] * (SOLVES - len(solves))
        updates += [(spare, k, k, 0)] * (UPDATES - len(updates))
        table.append([x for t in solves + updates for x in t])
    return np.array(table, np.int32)


def factor_panel(tile, store, inverse, beside):
    first_up, first_inv = factor_values(tile[:HALF, :HALF], beside)
    cross = exact(tile[HALF:, :HALF], first_inv, NT)
    rest = tile[HALF:, HALF:] - exact(cross, cross, NT)
    steps = HALF // 16
    second_up, second_inv = factor_values(rest, lambda j: beside(j + steps))
    corner = -exact(second_inv, exact(cross, first_inv, NN), NN)
    zero = jnp.zeros((HALF, HALF), F32)
    inverse[:HALF, :HALF] = first_inv
    inverse[:HALF, HALF:] = zero
    inverse[HALF:, :HALF] = corner
    inverse[HALF:, HALF:] = second_inv
    top = jnp.concatenate([first_up.T, zero], axis=1)
    bottom = jnp.concatenate([cross, second_up.T], axis=1)
    store(jnp.concatenate([top, bottom], axis=0))


def factor_range(plan_ref, work, high, low, inverses, wait, first, last):
    def solve(slot, i, k, to):
        value = exact(work[slot, i].reshape(PANEL, PANEL), inverses[k], NT)
        work[slot, i] = value.reshape(LANES, 8, PANEL)
        top, bottom = split(value)
        high[to, i] = top
        low[to, i] = bottom

    def update(slot, k, i, m):
        value = dot3(high[m, i], low[m, i], high[m, k], low[m, k]).reshape(LANES, 8, PANEL)
        work[slot, i] = work[slot, i] - value

    wait(jnp.int32(first))
    for m in range(first):
        update(0, first, first, m)

    def step(k, carry):
        at = k - first
        wait(k + 1)

        @pl.when(k > first)
        def _():
            solve(at - 1, k, k - 1, k - 1)
            update(at, k, k, k - 1)

        def item(j):
            if j < SOLVES:
                slot, i, to = (plan_ref[at, 3 * j + x] for x in range(3))
                solve(slot, i, jnp.maximum(k - 1, first), to)
            elif j < SOLVES + UPDATES:
                base = 3 * SOLVES + 4 * (j - SOLVES)
                update(*(plan_ref[at, base + x] for x in range(4)))

        def beside(step):
            item(2 * step)
            item(2 * step + 1)

        def store(value):
            work[at, k] = value.reshape(LANES, 8, PANEL)

        factor_panel(work[at, k].reshape(PANEL, PANEL), store, inverses.at[k], beside)
        return carry

    lax.fori_loop(first, last, step, 0)
    return solve


def own_rows(place_ref, own_ref, work, first, last):
    own_tile, own_group = place_ref[0], place_ref[1]
    for k in range(first, last):
        mine = work[k - first, own_tile, own_group]
        own_ref[:, k * PANEL : (k + 1) * PANEL] = jnp.where(own_tile >= k, mine, 0.0)


def early_kernel(place_ref, plan_ref, mine_ref, other_ref, own_ref, high_ref, low_ref, inverse_ref, work, high, low, sems):
    start_fetch(place_ref, mine_ref, other_ref, work, sems, 0, EARLY)
    wait = lambda k: wait_fetch(k, work, sems, 0, EARLY)
    solve = factor_range(plan_ref, work, high, low, inverse_ref, wait, 0, EARLY)
    last = EARLY - 1
    for i in range(EARLY, COUNT):
        solve(last, i, last, last)
    high_ref[...] = high[:EARLY]
    low_ref[...] = low[:EARLY]
    own_rows(place_ref, own_ref, work, 0, EARLY)


def late_kernel(
    place_ref, plan_ref, mine_ref, other_ref, high_ref, low_ref, inverse_ref, early_ref, cols_ref, trail_u_ref, trail_v_ref,
    own_ref, row_ref, col_ref, grown_u_ref, grown_v_ref,
    work, high, low, inverses, rows_all, pan, base, solved, change, sems, more_sems,
):
    x0, y0, core = place_ref[2], place_ref[3], place_ref[4]
    last = COUNT - 1
    loads = []
    for j in range(EARLY):
        loads.append(pltpu.make_async_copy(high_ref.at[j], high.at[j, pl.ds(0, COUNT)], more_sems.at[3 * j]))
        loads.append(pltpu.make_async_copy(low_ref.at[j], low.at[j, pl.ds(0, COUNT)], more_sems.at[3 * j + 1]))
        loads.append(pltpu.make_async_copy(inverse_ref.at[j], inverses.at[j], more_sems.at[3 * j + 2]))
    loads.append(pltpu.make_async_copy(cols_ref.at[1], pan.at[pl.ds(RANK, RANK)], more_sems.at[3 * EARLY]))
    for copy in loads:
        copy.start()
    tiles = tile_start(COUNT, EARLY)
    row_sem = more_sems.at[3 * EARLY + 1]
    for source, owner in ((mine_ref, core), (other_ref, 1 - core)):
        for outer in range(4):
            for inner in range(4):
                dx = jnp.where(owner == 0, outer, inner)
                dy = jnp.where(owner == 0, inner, outer)
                group = (lax.rem(x0 - dx + 4, 4) * 4 + lax.rem(y0 - dy + 4, 4)) * 2 + owner
                pltpu.make_async_copy(source.at[outer, inner, pl.ds(tiles, 4)], rows_all.at[:, group], row_sem).start()
    start_fetch(place_ref, mine_ref, other_ref, work, sems, EARLY, COUNT)
    passing = [
        pltpu.make_async_copy(trail_u_ref, grown_u_ref.at[pl.ds(0, RANK)], more_sems.at[3 * EARLY + 2]),
        pltpu.make_async_copy(trail_v_ref, grown_v_ref.at[pl.ds(0, RANK)], more_sems.at[3 * EARLY + 3]),
        pltpu.make_async_copy(cols_ref.at[0], grown_v_ref.at[pl.ds(RANK, RANK)], more_sems.at[3 * EARLY + 4]),
    ]
    for copy in passing:
        copy.start()
    for copy in loads:
        copy.wait()
    pltpu.make_async_copy(rows_all, rows_all, row_sem).wait()
    for k in range(COUNT):
        cols = slice(k * PANEL, (k + 1) * PANEL)
        for r in range(2):
            base[32 * r : 32 * r + 32, cols] = rows_all[r, :, k, :]
            pan[32 * r : 32 * r + 32, cols] = rows_all[2 + r, :, k, :]
    empty = jnp.zeros((LANES // 2, 8, PANEL), F32)
    nothing = jnp.zeros((HALF, PANEL), BF16)
    for k in range(COUNT):
        cols = slice(k * PANEL, (k + 1) * PANEL)
        value = pan[:, cols]
        if k < EARLY:
            for m in range(k):
                value = value - dot3(high[m, COUNT, :HALF], low[m, COUNT, :HALF], high[m, k], low[m, k])
            value = exact(value, inverses[k], NT)
            solved[:, cols] = value
            high[k, COUNT, :HALF], low[k, COUNT, :HALF] = split(value)
            high[k, COUNT, HALF:] = nothing
            low[k, COUNT, HALF:] = nothing
        else:
            work[k - EARLY, COUNT, : LANES // 2] = value.reshape(LANES // 2, 8, PANEL)
            work[k - EARLY, COUNT, LANES // 2 :] = empty
    wait = lambda k: wait_fetch(k, work, sems, EARLY, COUNT)
    solve = factor_range(plan_ref, work, high, low, inverses, wait, EARLY, COUNT)
    solve(last - EARLY, COUNT, last, last)
    for k in range(EARLY, COUNT):
        solved[:, k * PANEL : (k + 1) * PANEL] = work[k - EARLY, COUNT, : LANES // 2].reshape(HALF, PANEL)
    coupling = exact(solved[:RANK, :], solved[RANK:, :], NT)
    change[...] = -exact(coupling, base[...], TN)
    out = pltpu.make_async_copy(change, grown_u_ref.at[pl.ds(RANK, RANK)], more_sems.at[3 * EARLY + 5])
    out.start()
    own_ref[:, : EARLY * PANEL] = early_ref[...]
    own_rows(place_ref, own_ref, work, EARLY, COUNT)
    for r in range(2):
        row_ref[r : r + 1, :] = solved[pl.ds(32 * r + place_ref[1], 1), :]
    col_ref[...] = solved[pl.ds(pl.multiple_of(RANK + place_ref[0] * 8, 8), 8), :]
    for copy in passing:
        copy.wait()
    out.wait()


VMEM = pl.BlockSpec(memory_space=pltpu.VMEM)
SMEM = pl.BlockSpec(memory_space=pltpu.SMEM)
ANYWHERE = pl.BlockSpec(memory_space=pl.ANY)
ROOM = pltpu.CompilerParams(vmem_limit_bytes=60 * 1024 * 1024)


def early_step(place, mine, other):
    return pl.pallas_call(
        early_kernel,
        out_shape=(
            jax.ShapeDtypeStruct((8, EARLY * PANEL), F32),
            jax.ShapeDtypeStruct((EARLY, COUNT, PANEL, PANEL), BF16),
            jax.ShapeDtypeStruct((EARLY, COUNT, PANEL, PANEL), BF16),
            jax.ShapeDtypeStruct((EARLY, PANEL, PANEL), F32),
        ),
        in_specs=[SMEM, SMEM, ANYWHERE, ANYWHERE],
        out_specs=(VMEM, VMEM, VMEM, VMEM),
        scratch_shapes=[
            pltpu.VMEM((EARLY + 1, COUNT, LANES, 8, PANEL), F32),
            pltpu.VMEM((COUNT + 1, COUNT, PANEL, PANEL), BF16),
            pltpu.VMEM((COUNT + 1, COUNT, PANEL, PANEL), BF16),
            pltpu.SemaphoreType.DMA((EARLY,)),
        ],
        compiler_params=ROOM,
        cost_estimate=pl.CostEstimate(flops=30 * 10**9, bytes_accessed=80 * 10**6, transcendentals=0),
    )(place, jnp.asarray(plan(0, EARLY, COUNT)), mine, other)


def late_step(place, mine, other, high, low, inverse, early, cols, trail_u, trail_v):
    late = COUNT - EARLY
    return pl.pallas_call(
        late_kernel,
        out_shape=(
            jax.ShapeDtypeStruct((8, SIZE), F32),
            jax.ShapeDtypeStruct((2, SIZE), F32),
            jax.ShapeDtypeStruct((8, SIZE), F32),
            jax.ShapeDtypeStruct((2 * RANK, SIZE), F32),
            jax.ShapeDtypeStruct((2 * RANK, SIZE), F32),
        ),
        in_specs=[SMEM, SMEM] + [ANYWHERE] * 5 + [VMEM] + [ANYWHERE] * 3,
        out_specs=(VMEM, VMEM, VMEM, ANYWHERE, ANYWHERE),
        scratch_shapes=[
            pltpu.VMEM((late + 1, COUNT + 1, LANES, 8, PANEL), F32),
            pltpu.VMEM((COUNT + 1, COUNT + 1, PANEL, PANEL), BF16),
            pltpu.VMEM((COUNT + 1, COUNT + 1, PANEL, PANEL), BF16),
            pltpu.VMEM((COUNT, PANEL, PANEL), F32),
            pltpu.VMEM((4, 32, 8, PANEL), F32),
            pltpu.VMEM((2 * RANK, SIZE), F32),
            pltpu.VMEM((RANK, SIZE), F32),
            pltpu.VMEM((2 * RANK, SIZE), F32),
            pltpu.VMEM((RANK, SIZE), F32),
            pltpu.SemaphoreType.DMA((late,)),
            pltpu.SemaphoreType.DMA((3 * EARLY + 6,)),
        ],
        compiler_params=ROOM,
        cost_estimate=pl.CostEstimate(flops=80 * 10**9, bytes_accessed=300 * 10**6, transcendentals=0),
    )(place, jnp.asarray(plan(EARLY, COUNT, COUNT + 1)), mine, other, high, low, inverse, early, cols, trail_u, trail_v)


def column(x, y, core):
    return (x % 4 * 4 + y % 4) * 2 + core


def ring(shift, stage):
    pairs = []
    for x in range(4):
        for y in range(4):
            for core in range(2):
                along_y = stage == core
                target = column(x, y + shift, core) if along_y else column(x + shift, y, core)
                pairs.append((column(x, y, core), target))
    return pairs


def spread_parts(piece, stage):
    return [piece] + [lax.ppermute(piece, "col", ring(s, stage)) for s in (1, 2, 3)]


def spread(piece, stage):
    return jnp.stack(spread_parts(piece, stage))


def tiles_of(bands, first, last):
    return jnp.concatenate([bands[k, k:] for k in range(first, last)], axis=0)


def swap(piece):
    return lax.ppermute(piece, "col", [(i, i ^ 1) for i in range(32)])


def body(diag_tile, row_pan_u, row_pan_v, col_pan_u, col_pan_v, trail_u, trail_v):
    row = lax.axis_index("row")
    col = lax.axis_index("col")
    cols = lax.all_gather(jnp.stack([col_pan_u[0], col_pan_v[0]]), "row", axis=1, tiled=True)
    copies = jnp.broadcast_to(diag_tile[None], (COUNT, 8, SIZE))
    bands = lax.all_to_all(copies, "row", 0, 0)
    bands = bands.reshape(COUNT, 8, COUNT, PANEL).transpose(2, 0, 1, 3)
    rows = jnp.concatenate([row_pan_u[0], row_pan_v[0]], axis=0).reshape(4, COUNT, PANEL)
    early = tiles_of(bands, 0, EARLY)
    late = jnp.concatenate([tiles_of(bands, EARLY, COUNT), rows], axis=0)
    early = spread(early, 0)
    early, late = lax.optimization_barrier((early, late))
    early = spread(early, 1)
    late = spread(late, 0)
    early_other = swap(early)
    early, early_other, late = lax.optimization_barrier((early, early_other, late))
    late = spread_parts(late, 1)
    place = jnp.stack([row, col, col // 8, col // 2 % 4, col % 2]).astype(jnp.int32)
    own, high, low, inverse = early_step(place, early, early_other)
    late, cols, high = lax.optimization_barrier((late, cols, high))
    late = jnp.stack(late)
    late_other = swap(late)
    own, row_own, col_own, grown_u, grown_v = late_step(
        place, late, late_other, high, low, inverse, own, cols, trail_u[0, 0], trail_v[0, 0]
    )
    return (own, row_own[None], col_own[None], grown_u[None, None], grown_v[None, None])


def solution(mesh):
    placed = (
        P(("row", "col"), None),
        P("row", "col", None),
        P("row", "col", None),
        P("col", "row", None),
        P("col", "row", None),
        P("row", "col", None, None),
        P("row", "col", None, None),
    )
    return jax.shard_map(
        body,
        mesh=mesh,
        in_specs=placed,
        out_specs=(
            P(("row", "col"), None),
            P("row", "col", None),
            P("col", "row", None),
            P("row", "col", None, None),
            P("row", "col", None, None),
        ),
        check_vma=False,
    )
```

time: 367 us -> 205 us (0.56)
  waiting for transfers between devices: 211 us -> 27.1 us
  blocking collectives: 0 us -> 24.8 us
  starting transfers between devices: 0.12 us -> 22.9 us
  Pallas kernels: 126 us -> 106 us
  local copies, waits for them, and re-layouts: 9.42 us -> 5.69 us
    all_gather x2 -> x0, waiting for transfers between devices: 175 us -> none  [the longest x1 123 us: body(): diag = lax.all_gather(diag_tile, ('row', 'col'), axis=0, tiled=True)]
    all_gather x1, waiting for transfers between devices: 35.5 us -> 0.02 us  [body(): lax.all_gather(jnp.stack([col_pan_u[0], col_pan_v[0]]), 'row', axis=1, ti...]
    ppermute x0 -> x14, waiting for transfers between devices: none -> 27.1 us  [the longest x12 21.6 us: spread_parts(): lax.ppermute(piece, 'col', ring(s, stage))]
    all_to_all x0 -> x1, blocking collectives: none -> 24.8 us  [body(): bands = lax.all_to_all(copies, 'row', 0, 0)]
    ppermute x0 -> x14, starting transfers between devices: none -> 22.9 us  [the longest x12 15 us: spread_parts(): lax.ppermute(piece, 'col', ring(s, stage))]
    pallas_call x1 -> x2, Pallas kernels: 126 us -> 106 us  [the longest x1 78 us: late_step(): pl.pallas_call(late_kernel, out_shape=(jax.ShapeDtypeStruct((8, SIZE), F3...]
  transfers between devices with their start and end apart: 3 -> 15, of which waited for: 3 -> 7; matrix products, arithmetic and copies ran while one was open for 3% -> 1% of each run, Pallas kernels for 0% -> 14%
where the time goes in v2:
time: 205 us
  Pallas kernels  106 us (52%)
  waiting for transfers between devices  27.1 us (13%)
  blocking collectives  24.8 us (12%)
  starting transfers between devices  22.9 us (11%)
  between operations  14.3 us (7%)
  local copies, waits for them, and re-layouts  5.69 us (3%)
  other arithmetic  3.82 us (2%)
    pallas_call x1, Pallas kernels, late_step(): pl.pallas_call(late_kernel, out_shape=(jax.ShapeDtypeStruct((8, SIZE), F3...  78 us
    pallas_call x1, Pallas kernels, early_step(): pl.pallas_call(early_kernel, out_shape=(jax.ShapeDtypeStruct((8, EARLY *...  28.4 us
    all_to_all x1, blocking collectives, body(): bands = lax.all_to_all(copies, 'row', 0, 0)  24.8 us
    ppermute x12, waiting for transfers between devices, spread_parts(): lax.ppermute(piece, 'col', ring(s, stage))  21.6 us
    ppermute x12, starting transfers between devices, spread_parts(): lax.ppermute(piece, 'col', ring(s, stage))  15 us
    ppermute x2, starting transfers between devices, swap(): return lax.ppermute(piece, 'col', [(i, i ^ 1) for i in range(32)])  7.89 us
    ppermute x2, waiting for transfers between devices, swap(): return lax.ppermute(piece, 'col', [(i, i ^ 1) for i in range(32)])  5.48 us
    unnamed x23, local copies, waits for them, and re-layouts  4.13 us
  transfers between devices with their start and end apart: 15, of which 7 were waited for; matrix products, arithmetic and copies ran while one was open for 1% of the time, Pallas kernels for 14%

profile of v2, /device:TPU:1, one launch (start us, length us, event | category | flops | bytes accessed | tf_op | source)
XLA Modules:
  0.0 205.1 jit_solution(10266740896101067036)
XLA Ops:
  7.2 0.0 copy-start.5
  7.2 0.0 all-gather.2.cloned.1.call-start
  7.2 0.9 broadcast_in_dim.18
  8.1 24.8 %all_to_all.5 = f32[8,8,2048]{2,1,0:T(8,128)S(1)} all-to-all(f32[8,8,2048]{2,1,0:T(8,128)S(1)} %broadcast_in_dim.18), channel_id=1, replica_groups=mesh['row'=8,'col'=32] {'row'}, dimensions={0} | all-to-all | bytes 1048576 | tf_op jit(solution)/shard_map/all_to_all | solution.py:422
  33.0 2.8 %collective-permute-start.1 = (f32[15,8,256]{2,1,0:T(8,128)S(1)}, f32[15,8,256]{2,1,0:T(8,128)S(1)}, u32[]{:S(2)}, u32[]{:S(2)}) collective-permute-start(f32[15,8,256]{2,1,0:T(8,128)S(1)} %get-tuple-element.46), channel_id=1, source_target_pairs={{0,4},{1,17},{2,6},{3,19},{4,0},{5,21},{6,2},{7,23},{8,12},{9,25},... | collective-permute-start | bytes 368648 | tf_op jit(solution)/shard_map/ppermute | solution.py:402
  35.8 0.3 collective-permute-start
  36.2 2.4 %collective-permute-start.2 = (f32[15,8,256]{2,1,0:T(8,128)S(1)}, f32[15,8,256]{2,1,0:T(8,128)S(1)}, u32[]{:S(2)}, u32[]{:S(2)}) collective-permute-start(f32[15,8,256]{2,1,0:T(8,128)S(1)} %get-tuple-element.46), channel_id=1, source_target_pairs={{0,6},{1,25},{2,0},{3,27},{4,2},{5,29},{6,4},{7,31},{8,14},{9,1},{... | collective-permute-start | bytes 368648 | tf_op jit(solution)/shard_map/ppermute | solution.py:402
  38.6 0.0 collective-permute-done.1
  38.6 2.4 %collective-permute-done = f32[15,8,256]{2,1,0:T(8,128)S(1)} collective-permute-done((f32[15,8,256]{2,1,0:T(8,128)S(1)}, f32[15,8,256]{2,1,0:T(8,128)S(1)}, u32[]{:S(2)}, u32[]{:S(2)}) %collective-permute-start) | collective-permute-done | bytes 122912 | tf_op jit(solution)/shard_map/ppermute | solution.py:402
  41.1 0.0 collective-permute-done.2
  41.1 0.0 copy-start.3
  41.1 0.0 copy-start.4
  41.2 2.8 %collective-permute-start.5 = (f32[4,15,8,256]{3,2,1,0:T(8,128)S(1)}, f32[4,15,8,256]{3,2,1,0:T(8,128)S(1)}, u32[]{:S(2)}, u32[]{:S(2)}) collective-permute-start(f32[4,15,8,256]{3,2,1,0:T(8,128)S(1)} %pad_maximum_fusion.3), channel_id=1, source_target_pairs={{0,24},{1,7},{2,26},{3,1},{4,28},{5,3},{6,30},{7,5},{8,0},{9,15},{... | collective-permute-start | bytes 1474568 | tf_op jit(solution)/shard_map/ppermute | solution.py:402
  44.0 0.2 collective-permute-start.4
  44.2 0.7 collective-permute-start.3
  44.9 10.2 %collective-permute-done.5 = f32[4,15,8,256]{3,2,1,0:T(8,128)S(1)} collective-permute-done((f32[4,15,8,256]{3,2,1,0:T(8,128)S(1)}, f32[4,15,8,256]{3,2,1,0:T(8,128)S(1)}, u32[]{:S(2)}, u32[]{:S(2)}) %collective-permute-start.5) | collective-permute-done | bytes 491552 | tf_op jit(solution)/shard_map/ppermute | solution.py:402
  55.0 0.0 collective-permute-done.4
  55.0 3.6 %collective-permute-done.3 = f32[4,15,8,256]{3,2,1,0:T(8,128)S(1)} collective-permute-done((f32[4,15,8,256]{3,2,1,0:T(8,128)S(1)}, f32[4,15,8,256]{3,2,1,0:T(8,128)S(1)}, u32[]{:S(2)}, u32[]{:S(2)}) %collective-permute-start.3) | collective-permute-done | bytes 491552 | tf_op jit(solution)/shard_map/ppermute | solution.py:402
  58.6 0.1 pad_maximum_fusion.1.mine_ref
  58.8 4.8 %collective-permute-start.6 = (f32[4,4,15,8,256]{4,3,2,1,0:T(8,128)S(1)}, f32[4,4,15,8,256]{4,3,2,1,0:T(8,128)}, u32[]{:S(2)}, u32[]{:S(2)}) collective-permute-start(f32[4,4,15,8,256]{4,3,2,1,0:T(8,128)S(1)} %pad_maximum_fusion.1.mine_ref), channel_id=1, source_target_pairs={{0,1},{1,0},{2,3},{3,2},{4,5},{5,4},{6,7},{7,6},{8,9},{9,8},{10,11... | collective-permute-start | bytes 5898248 | tf_op jit(solution)/shard_map/ppermute | solution.py:414
  63.6 0.3 collective-permute-start.9
  63.9 1.3 collective-permute-start.8
  65.2 0.5 collective-permute-start.7
  65.7 0.0 copy-done.4
  65.7 0.7 pad_maximum_fusion.4
  66.4 0.0 all-gather.2.cloned.1.call-update
  66.5 0.6 stack.86.place_ref
  67.1 1.4 collective-permute-done.9
  68.5 1.6 collective-permute-done.8
  70.1 2.4 %collective-permute-done.7 = f32[25,8,256]{2,1,0:T(8,128)S(1)} collective-permute-done((f32[25,8,256]{2,1,0:T(8,128)S(1)}, f32[25,8,256]{2,1,0:T(8,128)S(1)}, u32[]{:S(2)}, u32[]{:S(2)}) %collective-permute-start.7) | collective-permute-done | bytes 204832 | tf_op jit(solution)/shard_map/ppermute | solution.py:402
  72.5 0.7 copy-done.2
  73.2 1.0 pad_maximum_fusion.2
  74.2 0.0 collective-permute-done.6.other_ref
  74.2 3.0 %collective-permute-start.12 = (f32[4,25,8,256]{3,2,1,0:T(8,128)S(1)}, f32[4,25,8,256]{3,2,1,0:T(8,128)}, u32[]{:S(2)}, u32[]{:S(2)}) collective-permute-start(f32[4,25,8,256]{3,2,1,0:T(8,128)S(1)} %pad_maximum_fusion.2), channel_id=1, source_target_pairs={{0,24},{1,7},{2,26},{3,1},{4,28},{5,3},{6,30},{7,5},{8,0},{9,15},{... | collective-permute-start | bytes 2457608 | tf_op jit(solution)/shard_map/ppermute | solution.py:402
  77.2 0.0 collective-permute-start.11
  77.2 0.7 collective-permute-start.10
  77.9 0.0 copy-done.1
  77.9 28.4 %shard_map.128 = (f32[8,512]{1,0:T(8,128)}, bf16[2,8,256,256]{3,2,1,0:T(8,128)(2,1)}, bf16[2,8,256,256]{3,2,1,0:T(8,128)(2,1)}, f32[2,256,256]{2,1,0:T(8,128)}) custom-call(s32[5]{0:T(128)} %stack.86.place_ref, s32[2,122]{1,0:T(2,128)} %constant.57.clone.plan_ref, f32[4,4,15,8,256]{4,3,2,1,0:T(8,128)} %copy-done.1, ...), custom_call_target="tpu_custom_call" | custom-call | flops 30000001024 | bytes 80000000 | tf_op jit(solution)/shard_map/pallas_call | solution.py:334
  106.3 0.0 all-gather.2.cloned.1.call-done.cols_ref
  106.3 0.0 collective-permute-done.12
  106.3 0.0 collective-permute-done.11
  106.3 0.0 collective-permute-done.10
  106.3 2.0 pad_maximum_fusion.mine_ref
  108.3 1.7 copy-done
  109.9 3.1 %collective-permute-start.13 = (f32[4,4,25,8,256]{4,3,2,1,0:T(8,128)S(1)}, f32[4,4,25,8,256]{4,3,2,1,0:T(8,128)S(1)}, u32[]{:S(2)}, u32[]{:S(2)}) collective-permute-start(f32[4,4,25,8,256]{4,3,2,1,0:T(8,128)S(1)} %pad_maximum_fusion.mine_ref), channel_id=1, source_target_pairs={{0,1},{1,0},{2,3},{3,2},{4,5},{5,4},{6,7},{7,6},{8,9},{9,8},{10,11... | collective-permute-start | bytes 9830408 | tf_op jit(solution)/shard_map/ppermute | solution.py:414
  113.0 5.5 %collective-permute-done.13.other_ref = f32[4,4,25,8,256]{4,3,2,1,0:T(8,128)S(1)} collective-permute-done((f32[4,4,25,8,256]{4,3,2,1,0:T(8,128)S(1)}, f32[4,4,25,8,256]{4,3,2,1,0:T(8,128)S(1)}, u32[]{:S(2)}, u32[]{:S(2)}) %collective-permute-start.13) | collective-permute-done | bytes 3276832 | tf_op jit(solution)/shard_map/ppermute | solution.py:414
  118.5 1.7 copy-done.7
  120.2 78.0 %shard_map.129 = (f32[8,2048]{1,0:T(8,128)}, f32[2,2048]{1,0:T(2,128)}, f32[8,2048]{1,0:T(8,128)}, f32[128,2048]{1,0:T(8,128)}, f32[128,2048]{1,0:T(8,128)}) custom-call(s32[5]{0:T(128)} %stack.86.place_ref, s32[6,122]{1,0:T(8,128)} %constant.58.clone.plan_ref, f32[4,4,25,8,256]{4,3,2,1,0:T(8,128)} %copy-done, f32[4,4,25,8,256]{4,3,2,1,0:T(8,128)} %copy-done.7, ...), custom_call_target="tpu_custom_call" | custom-call | flops 80000000000 | bytes 300000000 | tf_op jit(solution)/shard_map/pallas_call | solution.py:357
  (21 shorter events, 0.2 us)
Async XLA Ops:
  7.2 31.4 %copy-start.5 = (f32[1,2,2048]{2,1,0:T(2,128)S(1)}, f32[1,2,2048]{2,1,0:T(2,128)}, u32[]{:S(2)}) copy-start(f32[1,2,2048]{2,1,0:T(2,128)} %param.10) | copy-start | bytes 49156
  7.2 31.4 %copy-start.6 = (f32[1,2,2048]{2,1,0:T(2,128)S(1)}, f32[1,2,2048]{2,1,0:T(2,128)}, u32[]{:S(2)}) copy-start(f32[1,2,2048]{2,1,0:T(2,128)} %param.11) | copy-start | bytes 49156
  7.2 99.1 %all-gather.2.cloned.1.call-start = ((), (), s32[]{:S(2)}) async-start(), calls=%async_computation.1 | async-start | bytes 1179648 | tf_op jit(solution)/shard_map/all_gather | solution.py:420
  33.0 5.6 %collective-permute-start.1 = (f32[15,8,256]{2,1,0:T(8,128)S(1)}, f32[15,8,256]{2,1,0:T(8,128)S(1)}, u32[]{:S(2)}, u32[]{:S(2)}) collective-permute-start(f32[15,8,256]{2,1,0:T(8,128)S(1)} %get-tuple-element.46), channel_id=1, source_target_pairs={{0,4},{1,17},{2,6},{3,19},{4,0},{5,21},{6,2},{7,23},{8,12},{9,25},... | collective-permute-start | bytes 368648 | tf_op jit(solution)/shard_map/ppermute | solution.py:402
  35.8 5.2 %collective-permute-start = (f32[15,8,256]{2,1,0:T(8,128)S(1)}, f32[15,8,256]{2,1,0:T(8,128)S(1)}, u32[]{:S(2)}, u32[]{:S(2)}) collective-permute-start(f32[15,8,256]{2,1,0:T(8,128)S(1)} %get-tuple-element.46), channel_id=1, source_target_pairs={{0,2},{1,9},{2,4},{3,11},{4,6},{5,13},{6,0},{7,15},{8,10},{9,17},{... | collective-permute-start | bytes 368648 | tf_op jit(solution)/shard_map/ppermute | solution.py:402
  36.2 4.9 %collective-permute-start.2 = (f32[15,8,256]{2,1,0:T(8,128)S(1)}, f32[15,8,256]{2,1,0:T(8,128)S(1)}, u32[]{:S(2)}, u32[]{:S(2)}) collective-permute-start(f32[15,8,256]{2,1,0:T(8,128)S(1)} %get-tuple-element.46), channel_id=1, source_target_pairs={{0,6},{1,25},{2,0},{3,27},{4,2},{5,29},{6,4},{7,31},{8,14},{9,1},{... | collective-permute-start | bytes 368648 | tf_op jit(solution)/shard_map/ppermute | solution.py:402
  41.1 24.6 %copy-start.3 = (f32[1,8,2048]{2,1,0:T(8,128)S(1)}, f32[1,8,2048]{2,1,0:T(8,128)}, u32[]{:S(2)}) copy-start(f32[1,8,2048]{2,1,0:T(8,128)} %param.13) | copy-start | bytes 196612
  41.1 24.6 %copy-start.4 = (f32[1,8,2048]{2,1,0:T(8,128)S(1)}, f32[1,8,2048]{2,1,0:T(8,128)}, u32[]{:S(2)}) copy-start(f32[1,8,2048]{2,1,0:T(8,128)} %param.12) | copy-start | bytes 196612
  41.2 13.9 %collective-permute-start.5 = (f32[4,15,8,256]{3,2,1,0:T(8,128)S(1)}, f32[4,15,8,256]{3,2,1,0:T(8,128)S(1)}, u32[]{:S(2)}, u32[]{:S(2)}) collective-permute-start(f32[4,15,8,256]{3,2,1,0:T(8,128)S(1)} %pad_maximum_fusion.3), channel_id=1, source_target_pairs={{0,24},{1,7},{2,26},{3,1},{4,28},{5,3},{6,30},{7,5},{8,0},{9,15},{... | collective-permute-start | bytes 1474568 | tf_op jit(solution)/shard_map/ppermute | solution.py:402
  44.0 11.0 %collective-permute-start.4 = (f32[4,15,8,256]{3,2,1,0:T(8,128)S(1)}, f32[4,15,8,256]{3,2,1,0:T(8,128)S(1)}, u32[]{:S(2)}, u32[]{:S(2)}) collective-permute-start(f32[4,15,8,256]{3,2,1,0:T(8,128)S(1)} %pad_maximum_fusion.3), channel_id=1, source_target_pairs={{0,16},{1,5},{2,18},{3,7},{4,20},{5,1},{6,22},{7,3},{8,24},{9,13},... | collective-permute-start | bytes 1474568 | tf_op jit(solution)/shard_map/ppermute | solution.py:402
  44.2 14.5 %collective-permute-start.3 = (f32[4,15,8,256]{3,2,1,0:T(8,128)S(1)}, f32[4,15,8,256]{3,2,1,0:T(8,128)S(1)}, u32[]{:S(2)}, u32[]{:S(2)}) collective-permute-start(f32[4,15,8,256]{3,2,1,0:T(8,128)S(1)} %pad_maximum_fusion.3), channel_id=1, source_target_pairs={{0,8},{1,3},{2,10},{3,5},{4,12},{5,7},{6,14},{7,1},{8,16},{9,11},{... | collective-permute-start | bytes 1474568 | tf_op jit(solution)/shard_map/ppermute | solution.py:402
  58.7 19.1 %copy-start.1 = (f32[4,4,15,8,256]{4,3,2,1,0:T(8,128)}, f32[4,4,15,8,256]{4,3,2,1,0:T(8,128)S(1)}, u32[]{:S(2)}) copy-start(f32[4,4,15,8,256]{4,3,2,1,0:T(8,128)S(1)} %pad_maximum_fusion.1.mine_ref) | copy-start | bytes 5898244
  58.8 15.4 %collective-permute-start.6 = (f32[4,4,15,8,256]{4,3,2,1,0:T(8,128)S(1)}, f32[4,4,15,8,256]{4,3,2,1,0:T(8,128)}, u32[]{:S(2)}, u32[]{:S(2)}) collective-permute-start(f32[4,4,15,8,256]{4,3,2,1,0:T(8,128)S(1)} %pad_maximum_fusion.1.mine_ref), channel_id=1, source_target_pairs={{0,1},{1,0},{2,3},{3,2},{4,5},{5,4},{6,7},{7,6},{8,9},{9,8},{10,11... | collective-permute-start | bytes 5898248 | tf_op jit(solution)/shard_map/ppermute | solution.py:414
  63.6 4.9 %collective-permute-start.9 = (f32[25,8,256]{2,1,0:T(8,128)S(1)}, f32[25,8,256]{2,1,0:T(8,128)S(1)}, u32[]{:S(2)}, u32[]{:S(2)}) collective-permute-start(f32[25,8,256]{2,1,0:T(8,128)S(1)} %constant_dynamic-update-slice_fusion), channel_id=1, source_target_pairs={{0,6},{1,25},{2,0},{3,27},{4,2},{5,29},{6,4},{7,31},{8,14},{9,1},{... | collective-permute-start | bytes 614408 | tf_op jit(solution)/shard_map/ppermute | solution.py:402
  63.9 6.2 %collective-permute-start.8 = (f32[25,8,256]{2,1,0:T(8,128)S(1)}, f32[25,8,256]{2,1,0:T(8,128)S(1)}, u32[]{:S(2)}, u32[]{:S(2)}) collective-permute-start(f32[25,8,256]{2,1,0:T(8,128)S(1)} %constant_dynamic-update-slice_fusion), channel_id=1, source_target_pairs={{0,4},{1,17},{2,6},{3,19},{4,0},{5,21},{6,2},{7,23},{8,12},{9,25},... | collective-permute-start | bytes 614408 | tf_op jit(solution)/shard_map/ppermute | solution.py:402
  65.2 7.3 %collective-permute-start.7 = (f32[25,8,256]{2,1,0:T(8,128)S(1)}, f32[25,8,256]{2,1,0:T(8,128)S(1)}, u32[]{:S(2)}, u32[]{:S(2)}) collective-permute-start(f32[25,8,256]{2,1,0:T(8,128)S(1)} %constant_dynamic-update-slice_fusion), channel_id=1, source_target_pairs={{0,2},{1,9},{2,4},{3,11},{4,6},{5,13},{6,0},{7,15},{8,10},{9,17},{... | collective-permute-start | bytes 614408 | tf_op jit(solution)/shard_map/ppermute | solution.py:402
  72.5 0.7 copy-start.2
  74.2 32.1 %collective-permute-start.12 = (f32[4,25,8,256]{3,2,1,0:T(8,128)S(1)}, f32[4,25,8,256]{3,2,1,0:T(8,128)}, u32[]{:S(2)}, u32[]{:S(2)}) collective-permute-start(f32[4,25,8,256]{3,2,1,0:T(8,128)S(1)} %pad_maximum_fusion.2), channel_id=1, source_target_pairs={{0,24},{1,7},{2,26},{3,1},{4,28},{5,3},{6,30},{7,5},{8,0},{9,15},{... | collective-permute-start | bytes 2457608 | tf_op jit(solution)/shard_map/ppermute | solution.py:402
  77.2 29.1 %collective-permute-start.11 = (f32[4,25,8,256]{3,2,1,0:T(8,128)S(1)}, f32[4,25,8,256]{3,2,1,0:T(8,128)}, u32[]{:S(2)}, u32[]{:S(2)}) collective-permute-start(f32[4,25,8,256]{3,2,1,0:T(8,128)S(1)} %pad_maximum_fusion.2), channel_id=1, source_target_pairs={{0,16},{1,5},{2,18},{3,7},{4,20},{5,1},{6,22},{7,3},{8,24},{9,13},... | collective-permute-start | bytes 2457608 | tf_op jit(solution)/shard_map/ppermute | solution.py:402
  77.2 29.1 %collective-permute-start.10 = (f32[4,25,8,256]{3,2,1,0:T(8,128)S(1)}, f32[4,25,8,256]{3,2,1,0:T(8,128)}, u32[]{:S(2)}, u32[]{:S(2)}) collective-permute-start(f32[4,25,8,256]{3,2,1,0:T(8,128)S(1)} %pad_maximum_fusion.2), channel_id=1, source_target_pairs={{0,8},{1,3},{2,10},{3,5},{4,12},{5,7},{6,14},{7,1},{8,16},{9,11},{... | collective-permute-start | bytes 2457608 | tf_op jit(solution)/shard_map/ppermute | solution.py:402
  108.3 1.7 copy-start
  109.9 8.5 %collective-permute-start.13 = (f32[4,4,25,8,256]{4,3,2,1,0:T(8,128)S(1)}, f32[4,4,25,8,256]{4,3,2,1,0:T(8,128)S(1)}, u32[]{:S(2)}, u32[]{:S(2)}) collective-permute-start(f32[4,4,25,8,256]{4,3,2,1,0:T(8,128)S(1)} %pad_maximum_fusion.mine_ref), channel_id=1, source_target_pairs={{0,1},{1,0},{2,3},{3,2},{4,5},{5,4},{6,7},{7,6},{8,9},{9,8},{10,11... | collective-permute-start | bytes 9830408 | tf_op jit(solution)/shard_map/ppermute | solution.py:414
  118.5 1.7 copy-start.7
Sparse Core Ops, SparseCore 0:
  66.6 31.0 all-gather.1

commit v3 on v2

--- a/solution.py
+++ b/solution.py
@@ -1,3 +1,5 @@
+import functools
+
 import jax
 import jax.numpy as jnp
 import numpy as np
@@ -68,21 +70,24 @@
         beside(top // groups)
         rows = work[top : top + groups]
         eyes = side[top : top + groups]
+        near = range(top + groups, min(count, top + 2 * groups))
         cols = [[along_lanes(rows[a], 8 * top + k) for a in range(groups)] for k in range(width)]
-        below = {
-            i: [along_lanes(work[i], 8 * top + k) for k in range(width)]
-            for i in range(top + groups, count)
-        }
+        below = {i: [along_lanes(work[i], 8 * top + k) for k in range(width)] for i in near}
+        raw = jnp.concatenate(rows, axis=0)
         up = [jnp.zeros((8, size), F32)] * groups
         inv = [jnp.zeros((8, size), F32)] * groups
+        pivot = along_rows(cols[0][0], 0)
         for k in range(width):
             ka, ks = divmod(k, 8)
-            pivot = along_rows(cols[k][ka], ks)
             scale = 1.0 / pivot
             root = lax.rsqrt(pivot)
+            here = sub == ks
+            heads = {m: along_rows(cols[m][ka], ks) for m in range(k + 1, width)}
+            if k + 1 < width:
+                na, ns = divmod(k + 1, 8)
+                pivot = along_rows(cols[k + 1][na] - (cols[k][na] * heads[k + 1]) * scale, ns)
             row_k = along_rows(rows[ka], ks)
             eye_k = along_rows(eyes[ka], ks)
-            here = sub == ks
             up[ka] = jnp.where(here, row_k * root, up[ka])
             inv[ka] = jnp.where(here, eye_k * root, inv[ka])
             times = []
@@ -93,15 +98,27 @@
                 rows[a] = rows[a] - times[a] * row_k
                 eyes[a] = eyes[a] - times[a] * eye_k
             for m in range(k + 1, width):
-                col_m = along_rows(cols[m][ka], ks)
-                cols[m] = [cols[m][a] - times[a] * col_m for a in range(groups)]
+                cols[m] = [cols[m][a] - times[a] * heads[m] for a in range(groups)]
         upper[top : top + groups] = up
         inverse[top : top + groups] = inv
         row_all = [along_rows(rows[k // 8], k % 8) for k in range(width)]
         eye_all = [along_rows(eyes[k // 8], k % 8) for k in range(width)]
-        for i in range(top + groups, count):
+        for i in near:
             work[i] = work[i] - total([below[i][k] * row_all[k] for k in range(width)])
             side[i] = side[i] - total([below[i][k] * eye_all[k] for k in range(width)])
+        if top + 2 * groups < count:
+            both = [jnp.concatenate(rows, axis=0), jnp.concatenate(eyes, axis=0)]
+            raw_high, raw_low = split(raw)
+            high, low = split(jnp.concatenate(both, axis=1))
+            change = lax.dot_general(
+                jnp.concatenate([raw_high, raw_low, raw_high], axis=0),
+                jnp.concatenate([high, high, low], axis=0),
+                TN,
+                preferred_element_type=F32,
+            )
+            for i in range(top + 2 * groups, count):
+                work[i] = work[i] - change[8 * i : 8 * i + 8, :size]
+                side[i] = side[i] - change[8 * i : 8 * i + 8, size:]
     upper = [jnp.where(sub + 8 * i <= lane, upper[i], 0.0) for i in range(count)]
     inverse = [jnp.where(sub + 8 * i >= lane, inverse[i], 0.0) for i in range(count)]
     return jnp.concatenate(upper, axis=0), jnp.concatenate(inverse, axis=0)
@@ -143,26 +160,28 @@
             pltpu.make_async_copy(whole, whole, sems.at[j - first]).wait()
 
 
-SOLVES = 6
-UPDATES = 26
+SOLVES = 5
+UPDATES = 18
+STEPS = 2 * (HALF // 16)
 
 
 def plan(first, last, rows):
     spare = last - first
+    left = {(p, i, m) for p in range(first, last) for i in range(p, rows) for m in range(p)}
+    left -= {(first, first, m) for m in range(first)} | {(p, p, p - 1) for p in range(first, last)}
     table = []
     for k in range(first, last):
-        solves, updates = [], []
-        if k > first:
-            solves = [(k - 1 - first, i, k - 1) for i in range(k + 1, rows)]
-        for m in range(k if k == first else k - 1, -1, -1) if k == first else [k - 1]:
-            if m < k:
-                updates += [(k - first, k, i, m) for i in range(k + 1, rows)]
-        if k + 1 < last:
-            updates += [(k + 1 - first, k + 1, i, m) for i in range(k + 1, rows) for m in range(k)]
-        assert len(solves) <= SOLVES and len(updates) <= UPDATES
+        solves = [(k - 1 - first, i, k - 1) for i in range(k + 1, rows)] if k > first else []
+        ready = [t for t in left if t[2] < k and t[0] <= k + 1]
+        due = lambda t: (t[0] - (t[0] == t[1]), t)
+        taken = sorted(ready, key=due)[:UPDATES]
+        left -= set(taken)
+        assert len(solves) <= SOLVES and all(due(t)[0] > k for t in left)
+        updates = [(p - first, p, i, m) for p, i, m in taken]
         solves += [(spare, 0, COUNT)] * (SOLVES - len(solves))
         updates += [(spare, k, k, 0)] * (UPDATES - len(updates))
         table.append([x for t in solves + updates for x in t])
+    assert not left
     return np.array(table, np.int32)
 
 
@@ -195,38 +214,57 @@
         value = dot3(high[m, i], low[m, i], high[m, k], low[m, k]).reshape(LANES, 8, PANEL)
         work[slot, i] = work[slot, i] - value
 
-    wait(jnp.int32(first))
-    for m in range(first):
-        update(0, first, first, m)
-
-    def step(k, carry):
+    def step(k, at, items):
+        def beside(j):
+            share = lambda x: -(-x * len(items) // STEPS)
+            for item in items[share(j) : share(j + 1)]:
+                item()
+
+        def store(value):
+            work[at, k] = value.reshape(LANES, 8, PANEL)
+
+        factor_panel(work[at, k].reshape(PANEL, PANEL), store, inverses.at[k], beside)
+
+    def head(k, at):
+        solve(at - 1, k, k - 1, k - 1)
+        update(at, k, k, k - 1)
+
+    def early():
+        for k in range(first, last):
+            wait(jnp.int32(k))
+            items = []
+            if k > first:
+                head(k, k)
+                items = [functools.partial(solve, k - 1, i, k - 1, k - 1) for i in range(k + 1, COUNT)]
+                items += [functools.partial(update, k, k, i, k - 1) for i in range(k + 1, COUNT)]
+            step(k, k, items)
+
+    def late_step_of(k, carry):
         at = k - first
         wait(k + 1)
 
         @pl.when(k > first)
         def _():
-            solve(at - 1, k, k - 1, k - 1)
-            update(at, k, k, k - 1)
+            head(k, at)
 
         def item(j):
             if j < SOLVES:
                 slot, i, to = (plan_ref[at, 3 * j + x] for x in range(3))
                 solve(slot, i, jnp.maximum(k - 1, first), to)
-            elif j < SOLVES + UPDATES:
+            else:
                 base = 3 * SOLVES + 4 * (j - SOLVES)
                 update(*(plan_ref[at, base + x] for x in range(4)))
 
-        def beside(step):
-            item(2 * step)
-            item(2 * step + 1)
-
-        def store(value):
-            work[at, k] = value.reshape(LANES, 8, PANEL)
-
-        factor_panel(work[at, k].reshape(PANEL, PANEL), store, inverses.at[k], beside)
+        step(k, at, [functools.partial(item, j) for j in range(SOLVES + UPDATES)])
         return carry
 
-    lax.fori_loop(first, last, step, 0)
+    if plan_ref is None:
+        early()
+    else:
+        wait(jnp.int32(first))
+        for m in range(first):
+            update(0, first, first, m)
+        lax.fori_loop(first, last, late_step_of, 0)
     return solve
 
 
@@ -237,15 +275,13 @@
         own_ref[:, k * PANEL : (k + 1) * PANEL] = jnp.where(own_tile >= k, mine, 0.0)
 
 
-def early_kernel(place_ref, plan_ref, mine_ref, other_ref, own_ref, high_ref, low_ref, inverse_ref, work, high, low, sems):
+def early_kernel(place_ref, mine_ref, other_ref, own_ref, high, low, inverse_ref, work, sems):
     start_fetch(place_ref, mine_ref, other_ref, work, sems, 0, EARLY)
     wait = lambda k: wait_fetch(k, work, sems, 0, EARLY)
-    solve = factor_range(plan_ref, work, high, low, inverse_ref, wait, 0, EARLY)
+    solve = factor_range(None, work, high, low, inverse_ref, wait, 0, EARLY)
     last = EARLY - 1
     for i in range(EARLY, COUNT):
         solve(last, i, last, last)
-    high_ref[...] = high[:EARLY]
-    low_ref[...] = low[:EARLY]
     own_rows(place_ref, own_ref, work, 0, EARLY)
 
 
@@ -339,17 +375,15 @@
             jax.ShapeDtypeStruct((EARLY, COUNT, PANEL, PANEL), BF16),
             jax.ShapeDtypeStruct((EARLY, PANEL, PANEL), F32),
         ),
-        in_specs=[SMEM, SMEM, ANYWHERE, ANYWHERE],
+        in_specs=[SMEM, ANYWHERE, ANYWHERE],
         out_specs=(VMEM, VMEM, VMEM, VMEM),
         scratch_shapes=[
-            pltpu.VMEM((EARLY + 1, COUNT, LANES, 8, PANEL), F32),
-            pltpu.VMEM((COUNT + 1, COUNT, PANEL, PANEL), BF16),
-            pltpu.VMEM((COUNT + 1, COUNT, PANEL, PANEL), BF16),
+            pltpu.VMEM((EARLY, COUNT, LANES, 8, PANEL), F32),
             pltpu.SemaphoreType.DMA((EARLY,)),
         ],
         compiler_params=ROOM,
         cost_estimate=pl.CostEstimate(flops=30 * 10**9, bytes_accessed=80 * 10**6, transcendentals=0),
-    )(place, jnp.asarray(plan(0, EARLY, COUNT)), mine, other)
+    )(place, mine, other)
 
 
 def late_step(place, mine, other, high, low, inverse, early, cols, trail_u, trail_v):
@@ -422,15 +456,13 @@
     bands = lax.all_to_all(copies, "row", 0, 0)
     bands = bands.reshape(COUNT, 8, COUNT, PANEL).transpose(2, 0, 1, 3)
     rows = jnp.concatenate([row_pan_u[0], row_pan_v[0]], axis=0).reshape(4, COUNT, PANEL)
-    early = tiles_of(bands, 0, EARLY)
-    late = jnp.concatenate([tiles_of(bands, EARLY, COUNT), rows], axis=0)
-    early = spread(early, 0)
-    early, late = lax.optimization_barrier((early, late))
-    early = spread(early, 1)
-    late = spread(late, 0)
+    count = tile_start(EARLY, 0)
+    tiles = jnp.concatenate([tiles_of(bands, 0, EARLY), tiles_of(bands, EARLY, COUNT), rows], axis=0)
+    tiles = spread_parts(tiles, 0)
+    early = spread(jnp.stack([part[:count] for part in tiles]), 1)
     early_other = swap(early)
-    early, early_other, late = lax.optimization_barrier((early, early_other, late))
-    late = spread_parts(late, 1)
+    early, tiles = lax.optimization_barrier((early, tiles))
+    late = spread_parts(jnp.stack([part[count:] for part in tiles]), 1)
     place = jnp.stack([row, col, col // 8, col // 2 % 4, col % 2]).astype(jnp.int32)
     own, high, low, inverse = early_step(place, early, early_other)
     late, cols, high = lax.optimization_barrier((late, cols, high))

time: 205 us -> 190 us (0.927)
  Pallas kernels: 106 us -> 86.2 us
  waiting for transfers between devices: 27.1 us -> 35.5 us
  starting transfers between devices: 22.9 us -> 20.7 us
    pallas_call x1, Pallas kernels: 78 us -> 66 us  [late_step(): pl.pallas_call(late_kernel, out_shape=(jax.ShapeDtypeStruct((8, SIZE), F3...]
    all_gather x1, waiting for transfers between devices: 0.02 us -> 9.38 us  [body(): lax.all_gather(jnp.stack([col_pan_u[0], col_pan_v[0]]), 'row', axis=1, ti...]
    pallas_call x1, Pallas kernels: 28.4 us -> 20.2 us  [early_step(): pl.pallas_call(early_kernel, out_shape=(jax.ShapeDtypeStruct((8, EARLY *...]
    ppermute x12 -> x9, starting transfers between devices: 15 us -> 10.6 us  [spread_parts(): lax.ppermute(piece, 'col', ring(s, stage))]
    ppermute x2, starting transfers between devices: 7.89 us -> 10 us  [swap(): return lax.ppermute(piece, 'col', [(i, i ^ 1) for i in range(32)])]
    ppermute x12 -> x9, waiting for transfers between devices: 21.6 us -> 19.9 us  [spread_parts(): lax.ppermute(piece, 'col', ring(s, stage))]
  transfers between devices with their start and end apart: 15 -> 12, of which waited for: 7 -> 9; matrix products, arithmetic and copies ran while one was open for 1% -> 1% of each run, Pallas kernels for 14% -> 11%
where the time goes in v3:
time: 190 us; the launch traced here: 189 us
  Pallas kernels  86.2 us (45%)
  waiting for transfers between devices  35.5 us (19%)
  blocking collectives  24.8 us (13%)
  starting transfers between devices  20.7 us (11%)
  between operations  14.3 us (8%)
  local copies, waits for them, and re-layouts  5.05 us (3%)
  other arithmetic  2.82 us (1%)
    pallas_call x1, Pallas kernels, late_step(): pl.pallas_call(late_kernel, out_shape=(jax.ShapeDtypeStruct((8, SIZE), F3...  66 us
    all_to_all x1, blocking collectives, body(): bands = lax.all_to_all(copies, 'row', 0, 0)  24.8 us
    pallas_call x1, Pallas kernels, early_step(): pl.pallas_call(early_kernel, out_shape=(jax.ShapeDtypeStruct((8, EARLY *...  20.2 us
    ppermute x9, waiting for transfers between devices, spread_parts(): lax.ppermute(piece, 'col', ring(s, stage))  19.9 us
    ppermute x9, starting transfers between devices, spread_parts(): lax.ppermute(piece, 'col', ring(s, stage))  10.6 us
    ppermute x2, starting transfers between devices, swap(): return lax.ppermute(piece, 'col', [(i, i ^ 1) for i in range(32)])  10 us
    all_gather x1, waiting for transfers between devices, body(): lax.all_gather(jnp.stack([col_pan_u[0], col_pan_v[0]]), 'row', axis=1, ti...  9.38 us
    ppermute x2, waiting for transfers between devices, swap(): return lax.ppermute(piece, 'col', [(i, i ^ 1) for i in range(32)])  6.2 us
  transfers between devices with their start and end apart: 12, of which 9 were waited for; matrix products, arithmetic and copies ran while one was open for 1% of the time, Pallas kernels for 11%

profile of v3, /device:TPU:1, one launch (start us, length us, event | category | flops | bytes accessed | tf_op | source)
XLA Modules:
  0.0 189.3 jit_solution(13909170920081249351)
XLA Ops:
  7.2 0.0 copy-start.4
  7.2 0.0 copy-start.5
  7.2 0.0 all-gather.2.cloned.1.call-start
  7.2 0.9 broadcast_in_dim.18
  8.1 24.8 %all_to_all.5 = f32[8,8,2048]{2,1,0:T(8,128)S(1)} all-to-all(f32[8,8,2048]{2,1,0:T(8,128)S(1)} %broadcast_in_dim.18), channel_id=1, replica_groups=mesh['row'=8,'col'=32] {'row'}, dimensions={0} | all-to-all | bytes 1048576 | tf_op jit(solution)/shard_map/all_to_all | solution.py:456
  33.1 0.0 copy-done.4
  33.1 0.0 copy-done.5
  33.1 2.6 %collective-permute-start.2 = (f32[40,8,256]{2,1,0:T(8,128)S(1)}, f32[40,8,256]{2,1,0:T(8,128)S(1)}, u32[]{:S(2)}, u32[]{:S(2)}) collective-permute-start(f32[40,8,256]{2,1,0:T(8,128)S(1)} %constant_dynamic-update-slice_fusion), channel_id=1, source_target_pairs={{0,6},{1,25},{2,0},{3,27},{4,2},{5,29},{6,4},{7,31},{8,14},{9,1},{... | collective-permute-start | bytes 983048 | tf_op jit(solution)/shard_map/ppermute | solution.py:436
  35.7 0.5 collective-permute-start.1
  36.2 0.6 collective-permute-start
  36.8 6.4 %collective-permute-done.2 = f32[40,8,256]{2,1,0:T(8,128)S(1)} collective-permute-done((f32[40,8,256]{2,1,0:T(8,128)S(1)}, f32[40,8,256]{2,1,0:T(8,128)S(1)}, u32[]{:S(2)}, u32[]{:S(2)}) %collective-permute-start.2) | collective-permute-done | bytes 327712 | tf_op jit(solution)/shard_map/ppermute | solution.py:436
  43.2 0.2 collective-permute-done.1
  43.5 3.5 %collective-permute-done = f32[40,8,256]{2,1,0:T(8,128)S(1)} collective-permute-done((f32[40,8,256]{2,1,0:T(8,128)S(1)}, f32[40,8,256]{2,1,0:T(8,128)S(1)}, u32[]{:S(2)}, u32[]{:S(2)}) %collective-permute-start) | collective-permute-done | bytes 327712 | tf_op jit(solution)/shard_map/ppermute | solution.py:436
  46.9 0.1 fusion.4
  47.0 0.0 copy-start.2
  47.0 0.0 copy-start.3
  47.0 2.7 %collective-permute-start.4 = (f32[4,15,8,256]{3,2,1,0:T(8,128)S(1)}, f32[4,15,8,256]{3,2,1,0:T(8,128)S(1)}, u32[]{:S(2)}, u32[]{:S(2)}) collective-permute-start(f32[4,15,8,256]{3,2,1,0:T(8,128)S(1)} %get-tuple-element.46), channel_id=1, source_target_pairs={{0,16},{1,5},{2,18},{3,7},{4,20},{5,1},{6,22},{7,3},{8,24},{9,13},... | collective-permute-start | bytes 1474568 | tf_op jit(solution)/shard_map/ppermute | solution.py:436
  49.7 0.7 collective-permute-start.3
  50.4 2.0 %collective-permute-start.5 = (f32[4,15,8,256]{3,2,1,0:T(8,128)S(1)}, f32[4,15,8,256]{3,2,1,0:T(8,128)S(1)}, u32[]{:S(2)}, u32[]{:S(2)}) collective-permute-start(f32[4,15,8,256]{3,2,1,0:T(8,128)S(1)} %get-tuple-element.46), channel_id=1, source_target_pairs={{0,24},{1,7},{2,26},{3,1},{4,28},{5,3},{6,30},{7,5},{8,0},{9,15},{... | collective-permute-start | bytes 1474568 | tf_op jit(solution)/shard_map/ppermute | solution.py:436
  52.4 4.2 %collective-permute-done.4 = f32[4,15,8,256]{3,2,1,0:T(8,128)S(1)} collective-permute-done((f32[4,15,8,256]{3,2,1,0:T(8,128)S(1)}, f32[4,15,8,256]{3,2,1,0:T(8,128)S(1)}, u32[]{:S(2)}, u32[]{:S(2)}) %collective-permute-start.4) | collective-permute-done | bytes 491552 | tf_op jit(solution)/shard_map/ppermute | solution.py:436
  56.7 5.2 %collective-permute-done.3 = f32[4,15,8,256]{3,2,1,0:T(8,128)S(1)} collective-permute-done((f32[4,15,8,256]{3,2,1,0:T(8,128)S(1)}, f32[4,15,8,256]{3,2,1,0:T(8,128)S(1)}, u32[]{:S(2)}, u32[]{:S(2)}) %collective-permute-start.3) | collective-permute-done | bytes 491552 | tf_op jit(solution)/shard_map/ppermute | solution.py:436
  61.9 0.4 collective-permute-done.5
  62.3 0.1 pad_maximum_fusion.1.mine_ref
  62.4 0.0 copy-start.1
  62.4 5.6 %collective-permute-start.9 = (f32[4,4,15,8,256]{4,3,2,1,0:T(8,128)S(1)}, f32[4,4,15,8,256]{4,3,2,1,0:T(8,128)}, u32[]{:S(2)}, u32[]{:S(2)}) collective-permute-start(f32[4,4,15,8,256]{4,3,2,1,0:T(8,128)S(1)} %pad_maximum_fusion.1.mine_ref), channel_id=1, source_target_pairs={{0,1},{1,0},{2,3},{3,2},{4,5},{5,4},{6,7},{7,6},{8,9},{9,8},{10,11... | collective-permute-start | bytes 5898248 | tf_op jit(solution)/shard_map/ppermute | solution.py:448
  68.0 0.0 copy-done.2
  68.0 0.0 copy-done.3
  68.0 0.7 pad_maximum_fusion.4
  68.7 0.0 all-gather.2.cloned.1.call-update
  68.8 0.6 stack.86.place_ref
  69.4 0.1 pad_maximum_fusion.2
  69.5 0.4 collective-permute-start.8
  69.9 0.0 collective-permute-start.7
  69.9 1.1 collective-permute-start.6
  71.0 0.7 collective-permute-done.9.other_ref
  71.8 0.0 copy-done.1
  71.8 20.2 %shard_map.119 = (f32[8,512]{1,0:T(8,128)}, bf16[2,8,256,256]{3,2,1,0:T(8,128)(2,1)}, bf16[2,8,256,256]{3,2,1,0:T(8,128)(2,1)}, f32[2,256,256]{2,1,0:T(8,128)}) custom-call(s32[5]{0:T(128)} %stack.86.place_ref, f32[4,4,15,8,256]{4,3,2,1,0:T(8,128)} %copy-done.1, f32[4,4,15,8,256]{4,3,2,1,0:T(8,128)} %collective-permute-done.9.other_ref), custom_call_target="tpu_custom_call" | custom-call | flops 30000001024 | bytes 80000000 | tf_op jit(solution)/shard_map/pallas_call | solution.py:370
  91.9 9.4 %all-gather.2.cloned.1.call-done.cols_ref = f32[2,64,2048]{2,1,0:T(8,128)} async-done(((f32[2,8,2048]{2,1,0:T(8,128)}), f32[2,64,2048]{2,1,0:T(8,128)}) %all-gather.2.cloned.1.call-update) | async-done | bytes 1048592 | tf_op jit(solution)/shard_map/all_gather | solution.py:454
  101.3 0.0 collective-permute-done.8
  101.3 0.0 collective-permute-done.7
  101.3 0.0 collective-permute-done.6
  101.3 1.9 pad_maximum_fusion.mine_ref
  103.2 0.0 copy-start
  103.2 1.7 copy-done
  104.9 4.4 %collective-permute-start.10 = (f32[4,4,25,8,256]{4,3,2,1,0:T(8,128)S(1)}, f32[4,4,25,8,256]{4,3,2,1,0:T(8,128)S(1)}, u32[]{:S(2)}, u32[]{:S(2)}) collective-permute-start(f32[4,4,25,8,256]{4,3,2,1,0:T(8,128)S(1)} %pad_maximum_fusion.mine_ref), channel_id=1, source_target_pairs={{0,1},{1,0},{2,3},{3,2},{4,5},{5,4},{6,7},{7,6},{8,9},{9,8},{10,11... | collective-permute-start | bytes 9830408 | tf_op jit(solution)/shard_map/ppermute | solution.py:448
  109.2 5.5 %collective-permute-done.10.other_ref = f32[4,4,25,8,256]{4,3,2,1,0:T(8,128)S(1)} collective-permute-done((f32[4,4,25,8,256]{4,3,2,1,0:T(8,128)S(1)}, f32[4,4,25,8,256]{4,3,2,1,0:T(8,128)S(1)}, u32[]{:S(2)}, u32[]{:S(2)}) %collective-permute-start.10) | collective-permute-done | bytes 3276832 | tf_op jit(solution)/shard_map/ppermute | solution.py:448
  114.7 1.7 copy-done.6
  116.4 66.0 %shard_map.120 = (f32[8,2048]{1,0:T(8,128)}, f32[2,2048]{1,0:T(2,128)}, f32[8,2048]{1,0:T(8,128)}, f32[128,2048]{1,0:T(8,128)}, f32[128,2048]{1,0:T(8,128)}) custom-call(s32[5]{0:T(128)} %stack.86.place_ref, s32[6,87]{1,0:T(8,128)} %constant.55.clone.plan_ref, f32[4,4,25,8,256]{4,3,2,1,0:T(8,128)} %copy-done, f32[4,4,25,8,256]{4,3,2,1,0:T(8,128)} %copy-done.6, ...), custom_call_target="tpu_custom_call" | custom-call | flops 80000000000 | bytes 300000000 | tf_op jit(solution)/shard_map/pallas_call | solution.py:391
  (20 shorter events, 0.2 us)
Async XLA Ops:
  7.2 25.9 %copy-start.4 = (f32[1,2,2048]{2,1,0:T(2,128)S(1)}, f32[1,2,2048]{2,1,0:T(2,128)}, u32[]{:S(2)}) copy-start(f32[1,2,2048]{2,1,0:T(2,128)} %param.9) | copy-start | bytes 49156
  7.2 25.9 %copy-start.5 = (f32[1,2,2048]{2,1,0:T(2,128)S(1)}, f32[1,2,2048]{2,1,0:T(2,128)}, u32[]{:S(2)}) copy-start(f32[1,2,2048]{2,1,0:T(2,128)} %param.10) | copy-start | bytes 49156
  7.2 94.1 %all-gather.2.cloned.1.call-start = ((), (), s32[]{:S(2)}) async-start(), calls=%async_computation.1 | async-start | bytes 1179648 | tf_op jit(solution)/shard_map/all_gather | solution.py:454
  33.1 10.1 %collective-permute-start.2 = (f32[40,8,256]{2,1,0:T(8,128)S(1)}, f32[40,8,256]{2,1,0:T(8,128)S(1)}, u32[]{:S(2)}, u32[]{:S(2)}) collective-permute-start(f32[40,8,256]{2,1,0:T(8,128)S(1)} %constant_dynamic-update-slice_fusion), channel_id=1, source_target_pairs={{0,6},{1,25},{2,0},{3,27},{4,2},{5,29},{6,4},{7,31},{8,14},{9,1},{... | collective-permute-start | bytes 983048 | tf_op jit(solution)/shard_map/ppermute | solution.py:436
  35.7 7.8 %collective-permute-start.1 = (f32[40,8,256]{2,1,0:T(8,128)S(1)}, f32[40,8,256]{2,1,0:T(8,128)S(1)}, u32[]{:S(2)}, u32[]{:S(2)}) collective-permute-start(f32[40,8,256]{2,1,0:T(8,128)S(1)} %constant_dynamic-update-slice_fusion), channel_id=1, source_target_pairs={{0,4},{1,17},{2,6},{3,19},{4,0},{5,21},{6,2},{7,23},{8,12},{9,25},... | collective-permute-start | bytes 983048 | tf_op jit(solution)/shard_map/ppermute | solution.py:436
  36.2 10.7 %collective-permute-start = (f32[40,8,256]{2,1,0:T(8,128)S(1)}, f32[40,8,256]{2,1,0:T(8,128)S(1)}, u32[]{:S(2)}, u32[]{:S(2)}) collective-permute-start(f32[40,8,256]{2,1,0:T(8,128)S(1)} %constant_dynamic-update-slice_fusion), channel_id=1, source_target_pairs={{0,2},{1,9},{2,4},{3,11},{4,6},{5,13},{6,0},{7,15},{8,10},{9,17},{... | collective-permute-start | bytes 983048 | tf_op jit(solution)/shard_map/ppermute | solution.py:436
  47.0 21.0 %copy-start.2 = (f32[1,8,2048]{2,1,0:T(8,128)S(1)}, f32[1,8,2048]{2,1,0:T(8,128)}, u32[]{:S(2)}) copy-start(f32[1,8,2048]{2,1,0:T(8,128)} %param.12) | copy-start | bytes 196612
  47.0 21.0 %copy-start.3 = (f32[1,8,2048]{2,1,0:T(8,128)S(1)}, f32[1,8,2048]{2,1,0:T(8,128)}, u32[]{:S(2)}) copy-start(f32[1,8,2048]{2,1,0:T(8,128)} %param.11) | copy-start | bytes 196612
  47.0 9.6 %collective-permute-start.4 = (f32[4,15,8,256]{3,2,1,0:T(8,128)S(1)}, f32[4,15,8,256]{3,2,1,0:T(8,128)S(1)}, u32[]{:S(2)}, u32[]{:S(2)}) collective-permute-start(f32[4,15,8,256]{3,2,1,0:T(8,128)S(1)} %get-tuple-element.46), channel_id=1, source_target_pairs={{0,16},{1,5},{2,18},{3,7},{4,20},{5,1},{6,22},{7,3},{8,24},{9,13},... | collective-permute-start | bytes 1474568 | tf_op jit(solution)/shard_map/ppermute | solution.py:436
  49.7 12.1 %collective-permute-start.3 = (f32[4,15,8,256]{3,2,1,0:T(8,128)S(1)}, f32[4,15,8,256]{3,2,1,0:T(8,128)S(1)}, u32[]{:S(2)}, u32[]{:S(2)}) collective-permute-start(f32[4,15,8,256]{3,2,1,0:T(8,128)S(1)} %get-tuple-element.46), channel_id=1, source_target_pairs={{0,8},{1,3},{2,10},{3,5},{4,12},{5,7},{6,14},{7,1},{8,16},{9,11},{... | collective-permute-start | bytes 1474568 | tf_op jit(solution)/shard_map/ppermute | solution.py:436
  50.4 11.8 %collective-permute-start.5 = (f32[4,15,8,256]{3,2,1,0:T(8,128)S(1)}, f32[4,15,8,256]{3,2,1,0:T(8,128)S(1)}, u32[]{:S(2)}, u32[]{:S(2)}) collective-permute-start(f32[4,15,8,256]{3,2,1,0:T(8,128)S(1)} %get-tuple-element.46), channel_id=1, source_target_pairs={{0,24},{1,7},{2,26},{3,1},{4,28},{5,3},{6,30},{7,5},{8,0},{9,15},{... | collective-permute-start | bytes 1474568 | tf_op jit(solution)/shard_map/ppermute | solution.py:436
  62.4 9.4 %copy-start.1 = (f32[4,4,15,8,256]{4,3,2,1,0:T(8,128)}, f32[4,4,15,8,256]{4,3,2,1,0:T(8,128)S(1)}, u32[]{:S(2)}) copy-start(f32[4,4,15,8,256]{4,3,2,1,0:T(8,128)S(1)} %pad_maximum_fusion.1.mine_ref) | copy-start | bytes 5898244
  62.4 9.4 %collective-permute-start.9 = (f32[4,4,15,8,256]{4,3,2,1,0:T(8,128)S(1)}, f32[4,4,15,8,256]{4,3,2,1,0:T(8,128)}, u32[]{:S(2)}, u32[]{:S(2)}) collective-permute-start(f32[4,4,15,8,256]{4,3,2,1,0:T(8,128)S(1)} %pad_maximum_fusion.1.mine_ref), channel_id=1, source_target_pairs={{0,1},{1,0},{2,3},{3,2},{4,5},{5,4},{6,7},{7,6},{8,9},{9,8},{10,11... | collective-permute-start | bytes 5898248 | tf_op jit(solution)/shard_map/ppermute | solution.py:448
  69.5 31.8 %collective-permute-start.8 = (f32[4,25,8,256]{3,2,1,0:T(8,128)S(1)}, f32[4,25,8,256]{3,2,1,0:T(8,128)}, u32[]{:S(2)}, u32[]{:S(2)}) collective-permute-start(f32[4,25,8,256]{3,2,1,0:T(8,128)S(1)} %pad_maximum_fusion.2), channel_id=1, source_target_pairs={{0,24},{1,7},{2,26},{3,1},{4,28},{5,3},{6,30},{7,5},{8,0},{9,15},{... | collective-permute-start | bytes 2457608 | tf_op jit(solution)/shard_map/ppermute | solution.py:436
  69.9 31.4 %collective-permute-start.7 = (f32[4,25,8,256]{3,2,1,0:T(8,128)S(1)}, f32[4,25,8,256]{3,2,1,0:T(8,128)}, u32[]{:S(2)}, u32[]{:S(2)}) collective-permute-start(f32[4,25,8,256]{3,2,1,0:T(8,128)S(1)} %pad_maximum_fusion.2), channel_id=1, source_target_pairs={{0,16},{1,5},{2,18},{3,7},{4,20},{5,1},{6,22},{7,3},{8,24},{9,13},... | collective-permute-start | bytes 2457608 | tf_op jit(solution)/shard_map/ppermute | solution.py:436
  69.9 31.4 %collective-permute-start.6 = (f32[4,25,8,256]{3,2,1,0:T(8,128)S(1)}, f32[4,25,8,256]{3,2,1,0:T(8,128)}, u32[]{:S(2)}, u32[]{:S(2)}) collective-permute-start(f32[4,25,8,256]{3,2,1,0:T(8,128)S(1)} %pad_maximum_fusion.2), channel_id=1, source_target_pairs={{0,8},{1,3},{2,10},{3,5},{4,12},{5,7},{6,14},{7,1},{8,16},{9,11},{... | collective-permute-start | bytes 2457608 | tf_op jit(solution)/shard_map/ppermute | solution.py:436
  103.2 1.7 copy-start
  104.9 9.8 %collective-permute-start.10 = (f32[4,4,25,8,256]{4,3,2,1,0:T(8,128)S(1)}, f32[4,4,25,8,256]{4,3,2,1,0:T(8,128)S(1)}, u32[]{:S(2)}, u32[]{:S(2)}) collective-permute-start(f32[4,4,25,8,256]{4,3,2,1,0:T(8,128)S(1)} %pad_maximum_fusion.mine_ref), channel_id=1, source_target_pairs={{0,1},{1,0},{2,3},{3,2},{4,5},{5,4},{6,7},{7,6},{8,9},{9,8},{10,11... | collective-permute-start | bytes 9830408 | tf_op jit(solution)/shard_map/ppermute | solution.py:448
  114.7 1.7 copy-start.6
Sparse Core Ops, SparseCore 0:
  68.9 32.4 all-gather.1

commit v4 on v3

--- a/solution.py
+++ b/solution.py
@@ -286,7 +286,7 @@
 
 
 def late_kernel(
-    place_ref, plan_ref, mine_ref, other_ref, high_ref, low_ref, inverse_ref, early_ref, cols_ref, trail_u_ref, trail_v_ref,
+    place_ref, plan_ref, mine_ref, other_ref, high_ref, low_ref, inverse_ref, early_ref, cols_ref, cols_other_ref, trail_u_ref, trail_v_ref,
     own_ref, row_ref, col_ref, grown_u_ref, grown_v_ref,
     work, high, low, inverses, rows_all, pan, base, solved, change, sems, more_sems,
 ):
@@ -297,7 +297,6 @@
         loads.append(pltpu.make_async_copy(high_ref.at[j], high.at[j, pl.ds(0, COUNT)], more_sems.at[3 * j]))
         loads.append(pltpu.make_async_copy(low_ref.at[j], low.at[j, pl.ds(0, COUNT)], more_sems.at[3 * j + 1]))
         loads.append(pltpu.make_async_copy(inverse_ref.at[j], inverses.at[j], more_sems.at[3 * j + 2]))
-    loads.append(pltpu.make_async_copy(cols_ref.at[1], pan.at[pl.ds(RANK, RANK)], more_sems.at[3 * EARLY]))
     for copy in loads:
         copy.start()
     tiles = tile_start(COUNT, EARLY)
@@ -310,16 +309,26 @@
                 group = (lax.rem(x0 - dx + 4, 4) * 4 + lax.rem(y0 - dy + 4, 4)) * 2 + owner
                 pltpu.make_async_copy(source.at[outer, inner, pl.ds(tiles, 4)], rows_all.at[:, group], row_sem).start()
     start_fetch(place_ref, mine_ref, other_ref, work, sems, EARLY, COUNT)
+    column_pieces = []
+    for source, first_bit in ((cols_ref, 0), (cols_other_ref, 1)):
+        for second in range(2):
+            for third in range(2):
+                place = (place_ref[0] ^ (4 * third + 2 * second + first_bit)) * 8
+                column_pieces.append((source.at[second, third], pl.multiple_of(place, 8)))
+    col_sem, out_sem = more_sems.at[3 * EARLY], more_sems.at[3 * EARLY + 4]
+    for source, place in column_pieces:
+        pltpu.make_async_copy(source.at[1], pan.at[pl.ds(RANK + place, 8)], col_sem).start()
+        pltpu.make_async_copy(source.at[0], grown_v_ref.at[pl.ds(RANK + place, 8)], out_sem).start()
     passing = [
         pltpu.make_async_copy(trail_u_ref, grown_u_ref.at[pl.ds(0, RANK)], more_sems.at[3 * EARLY + 2]),
         pltpu.make_async_copy(trail_v_ref, grown_v_ref.at[pl.ds(0, RANK)], more_sems.at[3 * EARLY + 3]),
-        pltpu.make_async_copy(cols_ref.at[0], grown_v_ref.at[pl.ds(RANK, RANK)], more_sems.at[3 * EARLY + 4]),
     ]
     for copy in passing:
         copy.start()
     for copy in loads:
         copy.wait()
     pltpu.make_async_copy(rows_all, rows_all, row_sem).wait()
+    pltpu.make_async_copy(pan.at[pl.ds(RANK, RANK)], pan.at[pl.ds(RANK, RANK)], col_sem).wait()
     for k in range(COUNT):
         cols = slice(k * PANEL, (k + 1) * PANEL)
         for r in range(2):
@@ -357,6 +366,8 @@
     col_ref[...] = solved[pl.ds(pl.multiple_of(RANK + place_ref[0] * 8, 8), 8), :]
     for copy in passing:
         copy.wait()
+    whole = grown_v_ref.at[pl.ds(RANK, RANK)]
+    pltpu.make_async_copy(whole, whole, out_sem).wait()
     out.wait()
 
 
@@ -386,7 +397,7 @@
     )(place, mine, other)
 
 
-def late_step(place, mine, other, high, low, inverse, early, cols, trail_u, trail_v):
+def late_step(place, mine, other, high, low, inverse, early, cols, cols_other, trail_u, trail_v):
     late = COUNT - EARLY
     return pl.pallas_call(
         late_kernel,
@@ -397,7 +408,7 @@
             jax.ShapeDtypeStruct((2 * RANK, SIZE), F32),
             jax.ShapeDtypeStruct((2 * RANK, SIZE), F32),
         ),
-        in_specs=[SMEM, SMEM] + [ANYWHERE] * 5 + [VMEM] + [ANYWHERE] * 3,
+        in_specs=[SMEM, SMEM] + [ANYWHERE] * 5 + [VMEM] + [ANYWHERE] * 4,
         out_specs=(VMEM, VMEM, VMEM, ANYWHERE, ANYWHERE),
         scratch_shapes=[
             pltpu.VMEM((late + 1, COUNT + 1, LANES, 8, PANEL), F32),
@@ -414,7 +425,7 @@
         ],
         compiler_params=ROOM,
         cost_estimate=pl.CostEstimate(flops=80 * 10**9, bytes_accessed=300 * 10**6, transcendentals=0),
-    )(place, jnp.asarray(plan(EARLY, COUNT, COUNT + 1)), mine, other, high, low, inverse, early, cols, trail_u, trail_v)
+    )(place, jnp.asarray(plan(EARLY, COUNT, COUNT + 1)), mine, other, high, low, inverse, early, cols, cols_other, trail_u, trail_v)
 
 
 def column(x, y, core):
@@ -448,28 +459,37 @@
     return lax.ppermute(piece, "col", [(i, i ^ 1) for i in range(32)])
 
 
+def across(piece, bit):
+    return lax.ppermute(piece, "row", [(i, i ^ bit) for i in range(8)])
+
+
 def body(diag_tile, row_pan_u, row_pan_v, col_pan_u, col_pan_v, trail_u, trail_v):
     row = lax.axis_index("row")
     col = lax.axis_index("col")
-    cols = lax.all_gather(jnp.stack([col_pan_u[0], col_pan_v[0]]), "row", axis=1, tiled=True)
     copies = jnp.broadcast_to(diag_tile[None], (COUNT, 8, SIZE))
     bands = lax.all_to_all(copies, "row", 0, 0)
     bands = bands.reshape(COUNT, 8, COUNT, PANEL).transpose(2, 0, 1, 3)
     rows = jnp.concatenate([row_pan_u[0], row_pan_v[0]], axis=0).reshape(4, COUNT, PANEL)
     count = tile_start(EARLY, 0)
     tiles = jnp.concatenate([tiles_of(bands, 0, EARLY), tiles_of(bands, EARLY, COUNT), rows], axis=0)
+    cols = lax.optimization_barrier((jnp.stack([col_pan_u[0], col_pan_v[0]]), bands))[0]
+    cols = jnp.stack([cols, across(cols, 4)])
     tiles = spread_parts(tiles, 0)
+    tiles, cols = lax.optimization_barrier((tiles, cols))
+    cols = jnp.stack([cols, across(cols, 2)])
     early = spread(jnp.stack([part[:count] for part in tiles]), 1)
+    early, cols = lax.optimization_barrier((early, cols))
     early_other = swap(early)
+    cols_other = across(cols, 1)
     early, tiles = lax.optimization_barrier((early, tiles))
     late = spread_parts(jnp.stack([part[count:] for part in tiles]), 1)
     place = jnp.stack([row, col, col // 8, col // 2 % 4, col % 2]).astype(jnp.int32)
     own, high, low, inverse = early_step(place, early, early_other)
-    late, cols, high = lax.optimization_barrier((late, cols, high))
+    late, cols_other, high = lax.optimization_barrier((late, cols_other, high))
     late = jnp.stack(late)
     late_other = swap(late)
     own, row_own, col_own, grown_u, grown_v = late_step(
-        place, late, late_other, high, low, inverse, own, cols, trail_u[0, 0], trail_v[0, 0]
+        place, late, late_other, high, low, inverse, own, cols, cols_other, trail_u[0, 0], trail_v[0, 0]
     )
     return (own, row_own[None], col_own[None], grown_u[None, None], grown_v[None, None])
 

time: 190 us -> 174 us (0.916)
  blocking collectives: 24.8 us -> 0 us
  between operations: 14.3 us -> 1.13 us
  starting transfers between devices: 20.7 us -> 33.2 us
  waiting for transfers between devices: 35.5 us -> 42.1 us
    all_to_all x1 -> x0, blocking collectives: 24.8 us -> none  [body(): bands = lax.all_to_all(copies, 'row', 0, 0)]
    all_to_all x0 -> x1, waiting for transfers between devices: none -> 17.1 us  [body(): bands = lax.all_to_all(copies, 'row', 0, 0)]
    ppermute x9, waiting for transfers between devices: 19.9 us -> 8.39 us  [spread_parts(): lax.ppermute(piece, 'col', ring(s, stage))]
    ppermute x0 -> x3, waiting for transfers between devices: none -> 11.1 us  [across(): return lax.ppermute(piece, 'row', [(i, i ^ bit) for i in range(8)])]
    all_gather x1 -> x0, waiting for transfers between devices: 9.38 us -> none  [body(): lax.all_gather(jnp.stack([col_pan_u[0], col_pan_v[0]]), 'row', axis=1, ti...]
    all_to_all x0 -> x1, starting transfers between devices: none -> 9.01 us  [body(): bands = lax.all_to_all(copies, 'row', 0, 0)]
    ppermute x0 -> x3, starting transfers between devices: none -> 6.5 us  [across(): return lax.ppermute(piece, 'row', [(i, i ^ bit) for i in range(8)])]
    ppermute x2, starting transfers between devices: 10 us -> 7.13 us  [swap(): return lax.ppermute(piece, 'col', [(i, i ^ 1) for i in range(32)])]
  transfers between devices with their start and end apart: 12 -> 15, of which waited for: 9 -> 7; matrix products, arithmetic and copies ran while one was open for 1% -> 2% of each run, Pallas kernels for 11% -> 12%
where the time goes in v4:
time: 174 us; the launch traced here: 173 us
  Pallas kernels  86.4 us (50%)
  waiting for transfers between devices  42.1 us (24%)
  starting transfers between devices  33.2 us (19%)
  local copies, waits for them, and re-layouts  6.87 us (4%)
  other arithmetic  3.2 us (2%)
    pallas_call x1, Pallas kernels, late_step(): pl.pallas_call(late_kernel, out_shape=(jax.ShapeDtypeStruct((8, SIZE), F3...  66.3 us
    pallas_call x1, Pallas kernels, early_step(): pl.pallas_call(early_kernel, out_shape=(jax.ShapeDtypeStruct((8, EARLY *...  20.1 us
    all_to_all x1, waiting for transfers between devices, body(): bands = lax.all_to_all(copies, 'row', 0, 0)  17.1 us
    ppermute x3, waiting for transfers between devices, across(): return lax.ppermute(piece, 'row', [(i, i ^ bit) for i in range(8)])  11.1 us
    ppermute x9, starting transfers between devices, spread_parts(): lax.ppermute(piece, 'col', ring(s, stage))  10.6 us
    all_to_all x1, starting transfers between devices, body(): bands = lax.all_to_all(copies, 'row', 0, 0)  9.01 us
    ppermute x9, waiting for transfers between devices, spread_parts(): lax.ppermute(piece, 'col', ring(s, stage))  8.39 us
    ppermute x2, starting transfers between devices, swap(): return lax.ppermute(piece, 'col', [(i, i ^ 1) for i in range(32)])  7.13 us
  transfers between devices with their start and end apart: 15, of which 7 were waited for; matrix products, arithmetic and copies ran while one was open for 2% of the time, Pallas kernels for 12%

profile of v4, /device:TPU:1, one launch (start us, length us, event | category | flops | bytes accessed | tf_op | source)
XLA Modules:
  0.0 172.9 jit_solution(14620430904829519546)
XLA Ops:
  0.6 0.0 copy-start.5
  0.6 0.0 copy-start.6
  0.7 1.7 broadcast_in_dim.18
  2.3 9.0 %all-to-all-start = ((f32[8,8,2048]{2,1,0:T(8,128)}), f32[8,8,2048]{2,1,0:T(8,128)S(1)}, u32[]{:S(2)}, u32[]{:S(2)}) async-start(f32[8,8,2048]{2,1,0:T(8,128)} %broadcast_in_dim.18), calls=%async_computation | async-start | bytes 1048576 | tf_op jit(solution)/shard_map/all_to_all | solution.py:470
  11.3 0.9 pad_maximum_fusion.6
  12.2 17.1 %all-to-all-done = f32[8,8,2048]{2,1,0:T(8,128)S(1)} async-done(((f32[8,8,2048]{2,1,0:T(8,128)}), f32[8,8,2048]{2,1,0:T(8,128)S(1)}, u32[]{:S(2)}, u32[]{:S(2)}) %all-to-all-start) | async-done | bytes 524320 | tf_op jit(solution)/shard_map/all_to_all | solution.py:470
  29.4 0.1 collective-permute-start.3
  29.6 0.0 copy-done.5
  29.6 0.0 copy-done.6
  29.6 2.6 %collective-permute-start.2 = (f32[40,8,256]{2,1,0:T(8,128)S(1)}, f32[40,8,256]{2,1,0:T(8,128)S(1)}, u32[]{:S(2)}, u32[]{:S(2)}) collective-permute-start(f32[40,8,256]{2,1,0:T(8,128)S(1)} %constant_dynamic-update-slice_fusion), channel_id=1, source_target_pairs={{0,6},{1,25},{2,0},{3,27},{4,2},{5,29},{6,4},{7,31},{8,14},{9,1},{... | collective-permute-start | bytes 983048 | tf_op jit(solution)/shard_map/ppermute | solution.py:447
  32.2 0.5 collective-permute-start.1
  32.7 0.6 collective-permute-start
  33.3 6.7 %collective-permute-done.3 = f32[2,8,2048]{2,1,0:T(8,128)S(1)} collective-permute-done((f32[2,8,2048]{2,1,0:T(8,128)S(1)}, f32[2,8,2048]{2,1,0:T(8,128)S(1)}, u32[]{:S(2)}, u32[]{:S(2)}) %collective-permute-start.3) | collective-permute-done | bytes 131104 | tf_op jit(solution)/shard_map/ppermute | solution.py:463
  40.0 0.0 collective-permute-done.2
  40.0 0.0 collective-permute-done.1
  40.0 0.0 copy-start.3
  40.0 3.4 %collective-permute-done = f32[40,8,256]{2,1,0:T(8,128)S(1)} collective-permute-done((f32[40,8,256]{2,1,0:T(8,128)S(1)}, f32[40,8,256]{2,1,0:T(8,128)S(1)}, u32[]{:S(2)}, u32[]{:S(2)}) %collective-permute-start) | collective-permute-done | bytes 327712 | tf_op jit(solution)/shard_map/ppermute | solution.py:447
  43.4 1.1 collective-permute-start.7
  44.6 0.1 fusion.6
  44.7 2.7 %collective-permute-start.5 = (f32[4,15,8,256]{3,2,1,0:T(8,128)S(1)}, f32[4,15,8,256]{3,2,1,0:T(8,128)S(1)}, u32[]{:S(2)}, u32[]{:S(2)}) collective-permute-start(f32[4,15,8,256]{3,2,1,0:T(8,128)S(1)} %get-tuple-element.62), channel_id=1, source_target_pairs={{0,16},{1,5},{2,18},{3,7},{4,20},{5,1},{6,22},{7,3},{8,24},{9,13},... | collective-permute-start | bytes 1474568 | tf_op jit(solution)/shard_map/ppermute | solution.py:447
  47.4 0.4 collective-permute-start.4
  47.8 2.3 %collective-permute-start.6 = (f32[4,15,8,256]{3,2,1,0:T(8,128)S(1)}, f32[4,15,8,256]{3,2,1,0:T(8,128)S(1)}, u32[]{:S(2)}, u32[]{:S(2)}) collective-permute-start(f32[4,15,8,256]{3,2,1,0:T(8,128)S(1)} %get-tuple-element.62), channel_id=1, source_target_pairs={{0,24},{1,7},{2,26},{3,1},{4,28},{5,3},{6,30},{7,5},{8,0},{9,15},{... | collective-permute-start | bytes 1474568 | tf_op jit(solution)/shard_map/ppermute | solution.py:447
  50.1 4.5 %collective-permute-done.7 = f32[2,2,8,2048]{3,2,1,0:T(8,128)S(1)} collective-permute-done((f32[2,2,8,2048]{3,2,1,0:T(8,128)S(1)}, f32[2,2,8,2048]{3,2,1,0:T(8,128)S(1)}, u32[]{:S(2)}, u32[]{:S(2)}) %collective-permute-start.7) | collective-permute-done | bytes 262176 | tf_op jit(solution)/shard_map/ppermute | solution.py:463
  54.6 0.0 collective-permute-done.5
  54.6 4.9 %collective-permute-done.4 = f32[4,15,8,256]{3,2,1,0:T(8,128)S(1)} collective-permute-done((f32[4,15,8,256]{3,2,1,0:T(8,128)S(1)}, f32[4,15,8,256]{3,2,1,0:T(8,128)S(1)}, u32[]{:S(2)}, u32[]{:S(2)}) %collective-permute-start.4) | collective-permute-done | bytes 491552 | tf_op jit(solution)/shard_map/ppermute | solution.py:447
  59.5 0.1 collective-permute-done.6
  59.6 0.1 pad_maximum_fusion.1.mine_ref
  59.7 4.4 %collective-permute-start.12 = (f32[4,4,15,8,256]{4,3,2,1,0:T(8,128)S(1)}, f32[4,4,15,8,256]{4,3,2,1,0:T(8,128)}, u32[]{:S(2)}, u32[]{:S(2)}) collective-permute-start(f32[4,4,15,8,256]{4,3,2,1,0:T(8,128)S(1)} %pad_maximum_fusion.1.mine_ref), channel_id=1, source_target_pairs={{0,1},{1,0},{2,3},{3,2},{4,5},{5,4},{6,7},{7,6},{8,9},{9,8},{10,11... | collective-permute-start | bytes 5898248 | tf_op jit(solution)/shard_map/ppermute | solution.py:459
  64.1 0.6 stack.104.place_ref
  64.8 0.9 slice_bitcast_fusion.2
  65.7 0.9 slice_bitcast_fusion.1
  66.7 0.1 pad_maximum_fusion.2
  66.8 0.4 collective-permute-start.10
  67.2 0.3 collective-permute-start.9
  67.5 0.8 collective-permute-start.8
  68.3 5.3 %collective-permute-start.11 = (f32[2,2,2,8,2048]{4,3,2,1,0:T(8,128)S(1)}, f32[2,2,2,8,2048]{4,3,2,1,0:T(8,128)S(1)}, u32[]{:S(2)}, u32[]{:S(2)}) collective-permute-start(f32[2,2,2,8,2048]{4,3,2,1,0:T(8,128)S(1)} %pad_maximum_fusion.3.cols_ref), channel_id=1, source_target_pairs={{0,32},{32,0},{64,96},{96,64},{128,160},{160,128},{192,224},{224,1... | collective-permute-start | bytes 1572872 | tf_op jit(solution)/shard_map/ppermute | solution.py:463
  73.6 0.0 collective-permute-done.12.other_ref
  73.6 20.1 %shard_map.119 = (f32[8,512]{1,0:T(8,128)}, bf16[2,8,256,256]{3,2,1,0:T(8,128)(2,1)}, bf16[2,8,256,256]{3,2,1,0:T(8,128)(2,1)}, f32[2,256,256]{2,1,0:T(8,128)}) custom-call(s32[5]{0:T(128)} %stack.104.place_ref, f32[4,4,15,8,256]{4,3,2,1,0:T(8,128)} %copy-done.1, f32[4,4,15,8,256]{4,3,2,1,0:T(8,128)} %collective-permute-done.12.other_ref), custom_call_target="tpu_custom_call" | custom-call | flops 30000001024 | bytes 80000000 | tf_op jit(solution)/shard_map/pallas_call | solution.py:381
  93.8 0.0 collective-permute-done.11.cols_other_ref
  93.8 0.0 collective-permute-done.10
  93.8 0.0 collective-permute-done.9
  93.8 0.0 collective-permute-done.8
  93.8 0.8 copy-done.8
  94.6 2.0 %pad_maximum_fusion.mine_ref = f32[4,4,25,8,256]{4,3,2,1,0:T(8,128)S(1)} fusion(f32[1,4,25,8,256]{4,3,2,1,0:T(8,128)} %bitcast.33, f32[1,4,25,8,256]{4,3,2,1,0:T(8,128)} %bitcast.32, f32[1,4,25,8,256]{4,3,2,1,0:T(8,128)} %bitcast.31, f32[1,4,25,8,256]{4,3,2,1,0:T(8,128)S(1)} %bitcast.87), kind=kLoop, calls=%fused_computation | loop fusion | flops 2457600 | bytes 6553600 | tf_op jit(solution)/shard_map/stack | solution.py:489
  96.5 2.7 %collective-permute-start.13 = (f32[4,4,25,8,256]{4,3,2,1,0:T(8,128)S(1)}, f32[4,4,25,8,256]{4,3,2,1,0:T(8,128)S(1)}, u32[]{:S(2)}, u32[]{:S(2)}) collective-permute-start(f32[4,4,25,8,256]{4,3,2,1,0:T(8,128)S(1)} %pad_maximum_fusion.mine_ref), channel_id=1, source_target_pairs={{0,1},{1,0},{2,3},{3,2},{4,5},{5,4},{6,7},{7,6},{8,9},{9,8},{10,11... | collective-permute-start | bytes 9830408 | tf_op jit(solution)/shard_map/ppermute | solution.py:459
  99.3 5.5 %collective-permute-done.13.other_ref = f32[4,4,25,8,256]{4,3,2,1,0:T(8,128)S(1)} collective-permute-done((f32[4,4,25,8,256]{4,3,2,1,0:T(8,128)S(1)}, f32[4,4,25,8,256]{4,3,2,1,0:T(8,128)S(1)}, u32[]{:S(2)}, u32[]{:S(2)}) %collective-permute-start.13) | collective-permute-done | bytes 3276832 | tf_op jit(solution)/shard_map/ppermute | solution.py:459
  104.8 1.7 copy-done.7
  106.5 66.3 %shard_map.120 = (f32[8,2048]{1,0:T(8,128)}, f32[2,2048]{1,0:T(2,128)}, f32[8,2048]{1,0:T(8,128)}, f32[128,2048]{1,0:T(8,128)}, f32[128,2048]{1,0:T(8,128)}) custom-call(s32[5]{0:T(128)} %stack.104.place_ref, s32[6,87]{1,0:T(8,128)} %constant.55.clone.plan_ref, f32[4,4,25,8,256]{4,3,2,1,0:T(8,128)} %copy-done, f32[4,4,25,8,256]{4,3,2,1,0:T(8,128)} %copy-done.7, ...), custom_call_target="tpu_custom_call" | custom-call | flops 80000000000 | bytes 300000000 | tf_op jit(solution)/shard_map/pallas_call | solution.py:402
  (28 shorter events, 0.2 us)
Async XLA Ops:
  0.6 28.9 %copy-start.5 = (f32[1,2,2048]{2,1,0:T(2,128)S(1)}, f32[1,2,2048]{2,1,0:T(2,128)}, u32[]{:S(2)}) copy-start(f32[1,2,2048]{2,1,0:T(2,128)} %param.9) | copy-start | bytes 49156
  0.6 28.9 %copy-start.6 = (f32[1,2,2048]{2,1,0:T(2,128)S(1)}, f32[1,2,2048]{2,1,0:T(2,128)}, u32[]{:S(2)}) copy-start(f32[1,2,2048]{2,1,0:T(2,128)} %param.10) | copy-start | bytes 49156
  2.3 27.0 %all-to-all-start = ((f32[8,8,2048]{2,1,0:T(8,128)}), f32[8,8,2048]{2,1,0:T(8,128)S(1)}, u32[]{:S(2)}, u32[]{:S(2)}) async-start(f32[8,8,2048]{2,1,0:T(8,128)} %broadcast_in_dim.18), calls=%async_computation | async-start | bytes 1048576 | tf_op jit(solution)/shard_map/all_to_all | solution.py:470
  29.4 10.6 %collective-permute-start.3 = (f32[2,8,2048]{2,1,0:T(8,128)S(1)}, f32[2,8,2048]{2,1,0:T(8,128)S(1)}, u32[]{:S(2)}, u32[]{:S(2)}) collective-permute-start(f32[2,8,2048]{2,1,0:T(8,128)S(1)} %pad_maximum_fusion.6), channel_id=1, source_target_pairs={{0,128},{32,160},{64,192},{96,224},{128,0},{160,32},{192,64},{224,... | collective-permute-start | bytes 393224 | tf_op jit(solution)/shard_map/ppermute | solution.py:463
  29.6 10.4 %collective-permute-start.2 = (f32[40,8,256]{2,1,0:T(8,128)S(1)}, f32[40,8,256]{2,1,0:T(8,128)S(1)}, u32[]{:S(2)}, u32[]{:S(2)}) collective-permute-start(f32[40,8,256]{2,1,0:T(8,128)S(1)} %constant_dynamic-update-slice_fusion), channel_id=1, source_target_pairs={{0,6},{1,25},{2,0},{3,27},{4,2},{5,29},{6,4},{7,31},{8,14},{9,1},{... | collective-permute-start | bytes 983048 | tf_op jit(solution)/shard_map/ppermute | solution.py:447
  32.2 7.9 %collective-permute-start.1 = (f32[40,8,256]{2,1,0:T(8,128)S(1)}, f32[40,8,256]{2,1,0:T(8,128)S(1)}, u32[]{:S(2)}, u32[]{:S(2)}) collective-permute-start(f32[40,8,256]{2,1,0:T(8,128)S(1)} %constant_dynamic-update-slice_fusion), channel_id=1, source_target_pairs={{0,4},{1,17},{2,6},{3,19},{4,0},{5,21},{6,2},{7,23},{8,12},{9,25},... | collective-permute-start | bytes 983048 | tf_op jit(solution)/shard_map/ppermute | solution.py:447
  32.7 10.7 %collective-permute-start = (f32[40,8,256]{2,1,0:T(8,128)S(1)}, f32[40,8,256]{2,1,0:T(8,128)S(1)}, u32[]{:S(2)}, u32[]{:S(2)}) collective-permute-start(f32[40,8,256]{2,1,0:T(8,128)S(1)} %constant_dynamic-update-slice_fusion), channel_id=1, source_target_pairs={{0,2},{1,9},{2,4},{3,11},{4,6},{5,13},{6,0},{7,15},{8,10},{9,17},{... | collective-permute-start | bytes 983048 | tf_op jit(solution)/shard_map/ppermute | solution.py:447
  40.0 4.6 %copy-start.3 = (f32[40,8,256]{2,1,0:T(8,128)}, f32[40,8,256]{2,1,0:T(8,128)S(1)}, u32[]{:S(2)}) copy-start(f32[40,8,256]{2,1,0:T(8,128)S(1)} %collective-permute-done.1) | copy-start | bytes 983044
  43.4 1.2 copy-start.4
  43.4 11.1 %collective-permute-start.7 = (f32[2,2,8,2048]{3,2,1,0:T(8,128)S(1)}, f32[2,2,8,2048]{3,2,1,0:T(8,128)S(1)}, u32[]{:S(2)}, u32[]{:S(2)}) collective-permute-start(f32[2,2,8,2048]{3,2,1,0:T(8,128)S(1)} %pad_maximum_fusion.5), channel_id=1, source_target_pairs={{0,64},{32,96},{64,0},{96,32},{128,192},{160,224},{192,128},{224,1... | collective-permute-start | bytes 786440 | tf_op jit(solution)/shard_map/ppermute | solution.py:463
  44.7 9.9 %collective-permute-start.5 = (f32[4,15,8,256]{3,2,1,0:T(8,128)S(1)}, f32[4,15,8,256]{3,2,1,0:T(8,128)S(1)}, u32[]{:S(2)}, u32[]{:S(2)}) collective-permute-start(f32[4,15,8,256]{3,2,1,0:T(8,128)S(1)} %get-tuple-element.62), channel_id=1, source_target_pairs={{0,16},{1,5},{2,18},{3,7},{4,20},{5,1},{6,22},{7,3},{8,24},{9,13},... | collective-permute-start | bytes 1474568 | tf_op jit(solution)/shard_map/ppermute | solution.py:447
  47.4 12.1 %collective-permute-start.4 = (f32[4,15,8,256]{3,2,1,0:T(8,128)S(1)}, f32[4,15,8,256]{3,2,1,0:T(8,128)S(1)}, u32[]{:S(2)}, u32[]{:S(2)}) collective-permute-start(f32[4,15,8,256]{3,2,1,0:T(8,128)S(1)} %get-tuple-element.62), channel_id=1, source_target_pairs={{0,8},{1,3},{2,10},{3,5},{4,12},{5,7},{6,14},{7,1},{8,16},{9,11},{... | collective-permute-start | bytes 1474568 | tf_op jit(solution)/shard_map/ppermute | solution.py:447
  47.8 11.8 %collective-permute-start.6 = (f32[4,15,8,256]{3,2,1,0:T(8,128)S(1)}, f32[4,15,8,256]{3,2,1,0:T(8,128)S(1)}, u32[]{:S(2)}, u32[]{:S(2)}) collective-permute-start(f32[4,15,8,256]{3,2,1,0:T(8,128)S(1)} %get-tuple-element.62), channel_id=1, source_target_pairs={{0,24},{1,7},{2,26},{3,1},{4,28},{5,3},{6,30},{7,5},{8,0},{9,15},{... | collective-permute-start | bytes 1474568 | tf_op jit(solution)/shard_map/ppermute | solution.py:447
  54.6 13.8 %copy-start.2 = (f32[2,2,2,8,2048]{4,3,2,1,0:T(8,128)}, f32[2,2,2,8,2048]{4,3,2,1,0:T(8,128)S(1)}, u32[]{:S(2)}) copy-start(f32[2,2,2,8,2048]{4,3,2,1,0:T(8,128)S(1)} %pad_maximum_fusion.3.cols_ref) | copy-start | bytes 1572868
  59.7 13.9 %copy-start.1 = (f32[4,4,15,8,256]{4,3,2,1,0:T(8,128)}, f32[4,4,15,8,256]{4,3,2,1,0:T(8,128)S(1)}, u32[]{:S(2)}) copy-start(f32[4,4,15,8,256]{4,3,2,1,0:T(8,128)S(1)} %pad_maximum_fusion.1.mine_ref) | copy-start | bytes 5898244
  59.7 13.9 %collective-permute-start.12 = (f32[4,4,15,8,256]{4,3,2,1,0:T(8,128)S(1)}, f32[4,4,15,8,256]{4,3,2,1,0:T(8,128)}, u32[]{:S(2)}, u32[]{:S(2)}) collective-permute-start(f32[4,4,15,8,256]{4,3,2,1,0:T(8,128)S(1)} %pad_maximum_fusion.1.mine_ref), channel_id=1, source_target_pairs={{0,1},{1,0},{2,3},{3,2},{4,5},{5,4},{6,7},{7,6},{8,9},{9,8},{10,11... | collective-permute-start | bytes 5898248 | tf_op jit(solution)/shard_map/ppermute | solution.py:459
  66.8 27.0 %collective-permute-start.10 = (f32[4,25,8,256]{3,2,1,0:T(8,128)S(1)}, f32[4,25,8,256]{3,2,1,0:T(8,128)}, u32[]{:S(2)}, u32[]{:S(2)}) collective-permute-start(f32[4,25,8,256]{3,2,1,0:T(8,128)S(1)} %pad_maximum_fusion.2), channel_id=1, source_target_pairs={{0,24},{1,7},{2,26},{3,1},{4,28},{5,3},{6,30},{7,5},{8,0},{9,15},{... | collective-permute-start | bytes 2457608 | tf_op jit(solution)/shard_map/ppermute | solution.py:447
  67.2 26.6 %collective-permute-start.9 = (f32[4,25,8,256]{3,2,1,0:T(8,128)S(1)}, f32[4,25,8,256]{3,2,1,0:T(8,128)}, u32[]{:S(2)}, u32[]{:S(2)}) collective-permute-start(f32[4,25,8,256]{3,2,1,0:T(8,128)S(1)} %pad_maximum_fusion.2), channel_id=1, source_target_pairs={{0,16},{1,5},{2,18},{3,7},{4,20},{5,1},{6,22},{7,3},{8,24},{9,13},... | collective-permute-start | bytes 2457608 | tf_op jit(solution)/shard_map/ppermute | solution.py:447
  67.5 26.2 %collective-permute-start.8 = (f32[4,25,8,256]{3,2,1,0:T(8,128)S(1)}, f32[4,25,8,256]{3,2,1,0:T(8,128)}, u32[]{:S(2)}, u32[]{:S(2)}) collective-permute-start(f32[4,25,8,256]{3,2,1,0:T(8,128)S(1)} %pad_maximum_fusion.2), channel_id=1, source_target_pairs={{0,8},{1,3},{2,10},{3,5},{4,12},{5,7},{6,14},{7,1},{8,16},{9,11},{... | collective-permute-start | bytes 2457608 | tf_op jit(solution)/shard_map/ppermute | solution.py:447
  68.3 25.4 %collective-permute-start.11 = (f32[2,2,2,8,2048]{4,3,2,1,0:T(8,128)S(1)}, f32[2,2,2,8,2048]{4,3,2,1,0:T(8,128)S(1)}, u32[]{:S(2)}, u32[]{:S(2)}) collective-permute-start(f32[2,2,2,8,2048]{4,3,2,1,0:T(8,128)S(1)} %pad_maximum_fusion.3.cols_ref), channel_id=1, source_target_pairs={{0,32},{32,0},{64,96},{96,64},{128,160},{160,128},{192,224},{224,1... | collective-permute-start | bytes 1572872 | tf_op jit(solution)/shard_map/ppermute | solution.py:463
  93.8 0.8 copy-start.8
  96.5 9.9 %copy-start = (f32[4,4,25,8,256]{4,3,2,1,0:T(8,128)}, f32[4,4,25,8,256]{4,3,2,1,0:T(8,128)S(1)}, u32[]{:S(2)}) copy-start(f32[4,4,25,8,256]{4,3,2,1,0:T(8,128)S(1)} %pad_maximum_fusion.mine_ref) | copy-start | bytes 9830404
  96.5 8.2 %collective-permute-start.13 = (f32[4,4,25,8,256]{4,3,2,1,0:T(8,128)S(1)}, f32[4,4,25,8,256]{4,3,2,1,0:T(8,128)S(1)}, u32[]{:S(2)}, u32[]{:S(2)}) collective-permute-start(f32[4,4,25,8,256]{4,3,2,1,0:T(8,128)S(1)} %pad_maximum_fusion.mine_ref), channel_id=1, source_target_pairs={{0,1},{1,0},{2,3},{3,2},{4,5},{5,4},{6,7},{7,6},{8,9},{9,8},{10,11... | collective-permute-start | bytes 9830408 | tf_op jit(solution)/shard_map/ppermute | solution.py:459
  104.7 1.7 copy-start.7

commit v5 on v4

--- a/solution.py
+++ b/solution.py
@@ -193,10 +193,9 @@
     second_up, second_inv = factor_values(rest, lambda j: beside(j + steps))
     corner = -exact(second_inv, exact(cross, first_inv, NN), NN)
     zero = jnp.zeros((HALF, HALF), F32)
-    inverse[:HALF, :HALF] = first_inv
-    inverse[:HALF, HALF:] = zero
-    inverse[HALF:, :HALF] = corner
-    inverse[HALF:, HALF:] = second_inv
+    inv_top = jnp.concatenate([first_inv, zero], axis=1)
+    inv_bottom = jnp.concatenate([corner, second_inv], axis=1)
+    inverse[0], inverse[1] = split(jnp.concatenate([inv_top, inv_bottom], axis=0))
     top = jnp.concatenate([first_up.T, zero], axis=1)
     bottom = jnp.concatenate([cross, second_up.T], axis=1)
     store(jnp.concatenate([top, bottom], axis=0))
@@ -204,7 +203,7 @@
 
 def factor_range(plan_ref, work, high, low, inverses, wait, first, last):
     def solve(slot, i, k, to):
-        value = exact(work[slot, i].reshape(PANEL, PANEL), inverses[k], NT)
+        value = dot3(*split(work[slot, i].reshape(PANEL, PANEL)), inverses[k, 0], inverses[k, 1])
         work[slot, i] = value.reshape(LANES, 8, PANEL)
         top, bottom = split(value)
         high[to, i] = top
@@ -342,7 +341,7 @@
         if k < EARLY:
             for m in range(k):
                 value = value - dot3(high[m, COUNT, :HALF], low[m, COUNT, :HALF], high[m, k], low[m, k])
-            value = exact(value, inverses[k], NT)
+            value = dot3(*split(value), inverses[k, 0], inverses[k, 1])
             solved[:, cols] = value
             high[k, COUNT, :HALF], low[k, COUNT, :HALF] = split(value)
             high[k, COUNT, HALF:] = nothing
@@ -384,7 +383,7 @@
             jax.ShapeDtypeStruct((8, EARLY * PANEL), F32),
             jax.ShapeDtypeStruct((EARLY, COUNT, PANEL, PANEL), BF16),
             jax.ShapeDtypeStruct((EARLY, COUNT, PANEL, PANEL), BF16),
-            jax.ShapeDtypeStruct((EARLY, PANEL, PANEL), F32),
+            jax.ShapeDtypeStruct((EARLY, 2, PANEL, PANEL), BF16),
         ),
         in_specs=[SMEM, ANYWHERE, ANYWHERE],
         out_specs=(VMEM, VMEM, VMEM, VMEM),
@@ -414,7 +413,7 @@
             pltpu.VMEM((late + 1, COUNT + 1, LANES, 8, PANEL), F32),
             pltpu.VMEM((COUNT + 1, COUNT + 1, PANEL, PANEL), BF16),
             pltpu.VMEM((COUNT + 1, COUNT + 1, PANEL, PANEL), BF16),
-            pltpu.VMEM((COUNT, PANEL, PANEL), F32),
+            pltpu.VMEM((COUNT, 2, PANEL, PANEL), BF16),
             pltpu.VMEM((4, 32, 8, PANEL), F32),
             pltpu.VMEM((2 * RANK, SIZE), F32),
             pltpu.VMEM((RANK, SIZE), F32),

time: 174 us -> 163 us (0.937)
  Pallas kernels: 86.4 us -> 75.6 us
    pallas_call x1, Pallas kernels: 66.3 us -> 56.8 us  [late_step(): pl.pallas_call(late_kernel, out_shape=(jax.ShapeDtypeStruct((8, SIZE), F3...]
where the time goes in v5:
time: 163 us; the launch traced here: 162 us
  Pallas kernels  75.6 us (46%)
  waiting for transfers between devices  42.1 us (26%)
  starting transfers between devices  33.5 us (21%)
  local copies, waits for them, and re-layouts  6.87 us (4%)
  other arithmetic  3.2 us (2%)
    pallas_call x1, Pallas kernels, late_step(): pl.pallas_call(late_kernel, out_shape=(jax.ShapeDtypeStruct((8, SIZE), F3...  56.8 us
    pallas_call x1, Pallas kernels, early_step(): pl.pallas_call(early_kernel, out_shape=(jax.ShapeDtypeStruct((8, EARLY *...  18.8 us
    all_to_all x1, waiting for transfers between devices, body(): bands = lax.all_to_all(copies, 'row', 0, 0)  17.1 us
    ppermute x3, waiting for transfers between devices, across(): return lax.ppermute(piece, 'row', [(i, i ^ bit) for i in range(8)])  11.1 us
    ppermute x9, starting transfers between devices, spread_parts(): lax.ppermute(piece, 'col', ring(s, stage))  10.6 us
    all_to_all x1, starting transfers between devices, body(): bands = lax.all_to_all(copies, 'row', 0, 0)  9.01 us
    ppermute x9, waiting for transfers between devices, spread_parts(): lax.ppermute(piece, 'col', ring(s, stage))  8.39 us
    ppermute x2, starting transfers between devices, swap(): return lax.ppermute(piece, 'col', [(i, i ^ 1) for i in range(32)])  7.35 us
  transfers between devices with their start and end apart: 15, of which 7 were waited for; matrix products, arithmetic and copies ran while one was open for 2% of the time, Pallas kernels for 12%

profile of v5, /device:TPU:1, one launch (start us, length us, event | category | flops | bytes accessed | tf_op | source)
XLA Modules:
  0.0 162.4 jit_solution(9802935755872687505)
XLA Ops:
  0.6 0.0 copy-start.5
  0.6 0.0 copy-start.6
  0.7 1.7 %broadcast_in_dim.18 = f32[8,8,2048]{2,1,0:T(8,128)} broadcast(f32[8,2048]{1,0:T(8,128)} %param.8), dimensions={1,2} | broadcast | bytes 589824 | tf_op jit(solution)/shard_map/broadcast_in_dim | solution.py:468
  2.3 9.0 %all-to-all-start = ((f32[8,8,2048]{2,1,0:T(8,128)}), f32[8,8,2048]{2,1,0:T(8,128)S(1)}, u32[]{:S(2)}, u32[]{:S(2)}) async-start(f32[8,8,2048]{2,1,0:T(8,128)} %broadcast_in_dim.18), calls=%async_computation | async-start | bytes 1048576 | tf_op jit(solution)/shard_map/all_to_all | solution.py:469
  11.3 0.9 pad_maximum_fusion.6
  12.2 17.1 %all-to-all-done = f32[8,8,2048]{2,1,0:T(8,128)S(1)} async-done(((f32[8,8,2048]{2,1,0:T(8,128)}), f32[8,8,2048]{2,1,0:T(8,128)S(1)}, u32[]{:S(2)}, u32[]{:S(2)}) %all-to-all-start) | async-done | bytes 524320 | tf_op jit(solution)/shard_map/all_to_all | solution.py:469
  29.4 0.1 collective-permute-start.3
  29.6 0.0 copy-done.5
  29.6 2.6 %collective-permute-start.2 = (f32[40,8,256]{2,1,0:T(8,128)S(1)}, f32[40,8,256]{2,1,0:T(8,128)S(1)}, u32[]{:S(2)}, u32[]{:S(2)}) collective-permute-start(f32[40,8,256]{2,1,0:T(8,128)S(1)} %constant_dynamic-update-slice_fusion), channel_id=1, source_target_pairs={{0,6},{1,25},{2,0},{3,27},{4,2},{5,29},{6,4},{7,31},{8,14},{9,1},{... | collective-permute-start | bytes 983048 | tf_op jit(solution)/shard_map/ppermute | solution.py:446
  32.2 0.5 collective-permute-start.1
  32.7 0.6 collective-permute-start
  33.3 6.7 %collective-permute-done.3 = f32[2,8,2048]{2,1,0:T(8,128)S(1)} collective-permute-done((f32[2,8,2048]{2,1,0:T(8,128)S(1)}, f32[2,8,2048]{2,1,0:T(8,128)S(1)}, u32[]{:S(2)}, u32[]{:S(2)}) %collective-permute-start.3) | collective-permute-done | bytes 131104 | tf_op jit(solution)/shard_map/ppermute | solution.py:462
  40.0 0.0 collective-permute-done.2
  40.0 0.0 collective-permute-done.1
  40.0 0.0 copy-start.3
  40.0 3.4 %collective-permute-done = f32[40,8,256]{2,1,0:T(8,128)S(1)} collective-permute-done((f32[40,8,256]{2,1,0:T(8,128)S(1)}, f32[40,8,256]{2,1,0:T(8,128)S(1)}, u32[]{:S(2)}, u32[]{:S(2)}) %collective-permute-start) | collective-permute-done | bytes 327712 | tf_op jit(solution)/shard_map/ppermute | solution.py:446
  43.4 1.1 collective-permute-start.7
  44.6 0.1 fusion.6
  44.7 2.7 %collective-permute-start.5 = (f32[4,15,8,256]{3,2,1,0:T(8,128)S(1)}, f32[4,15,8,256]{3,2,1,0:T(8,128)S(1)}, u32[]{:S(2)}, u32[]{:S(2)}) collective-permute-start(f32[4,15,8,256]{3,2,1,0:T(8,128)S(1)} %get-tuple-element.62), channel_id=1, source_target_pairs={{0,16},{1,5},{2,18},{3,7},{4,20},{5,1},{6,22},{7,3},{8,24},{9,13},... | collective-permute-start | bytes 1474568 | tf_op jit(solution)/shard_map/ppermute | solution.py:446
  47.4 0.4 collective-permute-start.4
  47.8 2.3 %collective-permute-start.6 = (f32[4,15,8,256]{3,2,1,0:T(8,128)S(1)}, f32[4,15,8,256]{3,2,1,0:T(8,128)S(1)}, u32[]{:S(2)}, u32[]{:S(2)}) collective-permute-start(f32[4,15,8,256]{3,2,1,0:T(8,128)S(1)} %get-tuple-element.62), channel_id=1, source_target_pairs={{0,24},{1,7},{2,26},{3,1},{4,28},{5,3},{6,30},{7,5},{8,0},{9,15},{... | collective-permute-start | bytes 1474568 | tf_op jit(solution)/shard_map/ppermute | solution.py:446
  50.1 4.5 %collective-permute-done.7 = f32[2,2,8,2048]{3,2,1,0:T(8,128)S(1)} collective-permute-done((f32[2,2,8,2048]{3,2,1,0:T(8,128)S(1)}, f32[2,2,8,2048]{3,2,1,0:T(8,128)S(1)}, u32[]{:S(2)}, u32[]{:S(2)}) %collective-permute-start.7) | collective-permute-done | bytes 262176 | tf_op jit(solution)/shard_map/ppermute | solution.py:462
  54.6 0.0 collective-permute-done.5
  54.6 4.9 %collective-permute-done.4 = f32[4,15,8,256]{3,2,1,0:T(8,128)S(1)} collective-permute-done((f32[4,15,8,256]{3,2,1,0:T(8,128)S(1)}, f32[4,15,8,256]{3,2,1,0:T(8,128)S(1)}, u32[]{:S(2)}, u32[]{:S(2)}) %collective-permute-start.4) | collective-permute-done | bytes 491552 | tf_op jit(solution)/shard_map/ppermute | solution.py:446
  59.5 0.1 collective-permute-done.6
  59.6 0.1 pad_maximum_fusion.1.mine_ref
  59.7 4.4 %collective-permute-start.12 = (f32[4,4,15,8,256]{4,3,2,1,0:T(8,128)S(1)}, f32[4,4,15,8,256]{4,3,2,1,0:T(8,128)}, u32[]{:S(2)}, u32[]{:S(2)}) collective-permute-start(f32[4,4,15,8,256]{4,3,2,1,0:T(8,128)S(1)} %pad_maximum_fusion.1.mine_ref), channel_id=1, source_target_pairs={{0,1},{1,0},{2,3},{3,2},{4,5},{5,4},{6,7},{7,6},{8,9},{9,8},{10,11... | collective-permute-start | bytes 5898248 | tf_op jit(solution)/shard_map/ppermute | solution.py:458
  64.1 0.6 stack.104.place_ref
  64.8 0.9 slice_bitcast_fusion.2
  65.7 0.9 slice_bitcast_fusion.1
  66.7 0.1 pad_maximum_fusion.2
  66.8 0.4 collective-permute-start.10
  67.2 0.3 collective-permute-start.9
  67.5 0.8 collective-permute-start.8
  68.3 5.3 %collective-permute-start.11 = (f32[2,2,2,8,2048]{4,3,2,1,0:T(8,128)S(1)}, f32[2,2,2,8,2048]{4,3,2,1,0:T(8,128)S(1)}, u32[]{:S(2)}, u32[]{:S(2)}) collective-permute-start(f32[2,2,2,8,2048]{4,3,2,1,0:T(8,128)S(1)} %pad_maximum_fusion.3.cols_ref), channel_id=1, source_target_pairs={{0,32},{32,0},{64,96},{96,64},{128,160},{160,128},{192,224},{224,1... | collective-permute-start | bytes 1572872 | tf_op jit(solution)/shard_map/ppermute | solution.py:462
  73.6 0.0 collective-permute-done.12.other_ref
  73.6 18.8 %shard_map.119 = (f32[8,512]{1,0:T(8,128)}, bf16[2,8,256,256]{3,2,1,0:T(8,128)(2,1)}, bf16[2,8,256,256]{3,2,1,0:T(8,128)(2,1)}, bf16[2,2,256,256]{3,2,1,0:T(8,128)(2,1)}) custom-call(s32[5]{0:T(128)} %stack.104.place_ref, f32[4,4,15,8,256]{4,3,2,1,0:T(8,128)} %copy-done.1, f32[4,4,15,8,256]{4,3,2,1,0:T(8,128)} %collective-permute-done.12.other_ref), custom_call_target="tpu_custom_call" | custom-call | flops 30000001024 | bytes 80000000 | tf_op jit(solution)/shard_map/pallas_call | solution.py:380
  92.4 0.0 collective-permute-done.11.cols_other_ref
  92.5 0.0 copy-start.8
  92.5 0.0 collective-permute-done.10
  92.5 0.0 collective-permute-done.9
  92.5 0.0 collective-permute-done.8
  92.5 0.8 copy-done.8
  93.3 2.0 %pad_maximum_fusion.mine_ref = f32[4,4,25,8,256]{4,3,2,1,0:T(8,128)S(1)} fusion(f32[1,4,25,8,256]{4,3,2,1,0:T(8,128)} %bitcast.33, f32[1,4,25,8,256]{4,3,2,1,0:T(8,128)} %bitcast.32, f32[1,4,25,8,256]{4,3,2,1,0:T(8,128)} %bitcast.31, f32[1,4,25,8,256]{4,3,2,1,0:T(8,128)S(1)} %bitcast.87), kind=kLoop, calls=%fused_computation | loop fusion | flops 2457600 | bytes 6553600 | tf_op jit(solution)/shard_map/stack | solution.py:488
  95.2 3.0 %collective-permute-start.13 = (f32[4,4,25,8,256]{4,3,2,1,0:T(8,128)S(1)}, f32[4,4,25,8,256]{4,3,2,1,0:T(8,128)S(1)}, u32[]{:S(2)}, u32[]{:S(2)}) collective-permute-start(f32[4,4,25,8,256]{4,3,2,1,0:T(8,128)S(1)} %pad_maximum_fusion.mine_ref), channel_id=1, source_target_pairs={{0,1},{1,0},{2,3},{3,2},{4,5},{5,4},{6,7},{7,6},{8,9},{9,8},{10,11... | collective-permute-start | bytes 9830408 | tf_op jit(solution)/shard_map/ppermute | solution.py:458
  98.2 5.5 %collective-permute-done.13.other_ref = f32[4,4,25,8,256]{4,3,2,1,0:T(8,128)S(1)} collective-permute-done((f32[4,4,25,8,256]{4,3,2,1,0:T(8,128)S(1)}, f32[4,4,25,8,256]{4,3,2,1,0:T(8,128)S(1)}, u32[]{:S(2)}, u32[]{:S(2)}) %collective-permute-start.13) | collective-permute-done | bytes 3276832 | tf_op jit(solution)/shard_map/ppermute | solution.py:458
  103.7 1.7 %copy-done.7 = f32[4,4,25,8,256]{4,3,2,1,0:T(8,128)} copy-done((f32[4,4,25,8,256]{4,3,2,1,0:T(8,128)}, f32[4,4,25,8,256]{4,3,2,1,0:T(8,128)S(1)}, u32[]{:S(2)}) %copy-start.7) | copy-done | bytes 3276824
  105.4 56.8 %shard_map.120 = (f32[8,2048]{1,0:T(8,128)}, f32[2,2048]{1,0:T(2,128)}, f32[8,2048]{1,0:T(8,128)}, f32[128,2048]{1,0:T(8,128)}, f32[128,2048]{1,0:T(8,128)}) custom-call(s32[5]{0:T(128)} %stack.104.place_ref, s32[6,87]{1,0:T(8,128)} %constant.55.clone.plan_ref, f32[4,4,25,8,256]{4,3,2,1,0:T(8,128)} %copy-done, f32[4,4,25,8,256]{4,3,2,1,0:T(8,128)} %copy-done.7, ...), custom_call_target="tpu_custom_call" | custom-call | flops 80000000000 | bytes 300000000 | tf_op jit(solution)/shard_map/pallas_call | solution.py:401
  (28 shorter events, 0.2 us)
Async XLA Ops:
  0.6 28.9 %copy-start.5 = (f32[1,2,2048]{2,1,0:T(2,128)S(1)}, f32[1,2,2048]{2,1,0:T(2,128)}, u32[]{:S(2)}) copy-start(f32[1,2,2048]{2,1,0:T(2,128)} %param.9) | copy-start | bytes 49156
  0.6 28.9 %copy-start.6 = (f32[1,2,2048]{2,1,0:T(2,128)S(1)}, f32[1,2,2048]{2,1,0:T(2,128)}, u32[]{:S(2)}) copy-start(f32[1,2,2048]{2,1,0:T(2,128)} %param.10) | copy-start | bytes 49156
  2.3 27.0 %all-to-all-start = ((f32[8,8,2048]{2,1,0:T(8,128)}), f32[8,8,2048]{2,1,0:T(8,128)S(1)}, u32[]{:S(2)}, u32[]{:S(2)}) async-start(f32[8,8,2048]{2,1,0:T(8,128)} %broadcast_in_dim.18), calls=%async_computation | async-start | bytes 1048576 | tf_op jit(solution)/shard_map/all_to_all | solution.py:469
  29.4 10.6 %collective-permute-start.3 = (f32[2,8,2048]{2,1,0:T(8,128)S(1)}, f32[2,8,2048]{2,1,0:T(8,128)S(1)}, u32[]{:S(2)}, u32[]{:S(2)}) collective-permute-start(f32[2,8,2048]{2,1,0:T(8,128)S(1)} %pad_maximum_fusion.6), channel_id=1, source_target_pairs={{0,128},{32,160},{64,192},{96,224},{128,0},{160,32},{192,64},{224,... | collective-permute-start | bytes 393224 | tf_op jit(solution)/shard_map/ppermute | solution.py:462
  29.6 10.4 %collective-permute-start.2 = (f32[40,8,256]{2,1,0:T(8,128)S(1)}, f32[40,8,256]{2,1,0:T(8,128)S(1)}, u32[]{:S(2)}, u32[]{:S(2)}) collective-permute-start(f32[40,8,256]{2,1,0:T(8,128)S(1)} %constant_dynamic-update-slice_fusion), channel_id=1, source_target_pairs={{0,6},{1,25},{2,0},{3,27},{4,2},{5,29},{6,4},{7,31},{8,14},{9,1},{... | collective-permute-start | bytes 983048 | tf_op jit(solution)/shard_map/ppermute | solution.py:446
  32.2 7.9 %collective-permute-start.1 = (f32[40,8,256]{2,1,0:T(8,128)S(1)}, f32[40,8,256]{2,1,0:T(8,128)S(1)}, u32[]{:S(2)}, u32[]{:S(2)}) collective-permute-start(f32[40,8,256]{2,1,0:T(8,128)S(1)} %constant_dynamic-update-slice_fusion), channel_id=1, source_target_pairs={{0,4},{1,17},{2,6},{3,19},{4,0},{5,21},{6,2},{7,23},{8,12},{9,25},... | collective-permute-start | bytes 983048 | tf_op jit(solution)/shard_map/ppermute | solution.py:446
  32.7 10.7 %collective-permute-start = (f32[40,8,256]{2,1,0:T(8,128)S(1)}, f32[40,8,256]{2,1,0:T(8,128)S(1)}, u32[]{:S(2)}, u32[]{:S(2)}) collective-permute-start(f32[40,8,256]{2,1,0:T(8,128)S(1)} %constant_dynamic-update-slice_fusion), channel_id=1, source_target_pairs={{0,2},{1,9},{2,4},{3,11},{4,6},{5,13},{6,0},{7,15},{8,10},{9,17},{... | collective-permute-start | bytes 983048 | tf_op jit(solution)/shard_map/ppermute | solution.py:446
  40.0 4.6 %copy-start.3 = (f32[40,8,256]{2,1,0:T(8,128)}, f32[40,8,256]{2,1,0:T(8,128)S(1)}, u32[]{:S(2)}) copy-start(f32[40,8,256]{2,1,0:T(8,128)S(1)} %collective-permute-done.1) | copy-start | bytes 983044
  43.4 1.2 copy-start.4
  43.4 11.1 %collective-permute-start.7 = (f32[2,2,8,2048]{3,2,1,0:T(8,128)S(1)}, f32[2,2,8,2048]{3,2,1,0:T(8,128)S(1)}, u32[]{:S(2)}, u32[]{:S(2)}) collective-permute-start(f32[2,2,8,2048]{3,2,1,0:T(8,128)S(1)} %pad_maximum_fusion.5), channel_id=1, source_target_pairs={{0,64},{32,96},{64,0},{96,32},{128,192},{160,224},{192,128},{224,1... | collective-permute-start | bytes 786440 | tf_op jit(solution)/shard_map/ppermute | solution.py:462
  44.7 9.9 %collective-permute-start.5 = (f32[4,15,8,256]{3,2,1,0:T(8,128)S(1)}, f32[4,15,8,256]{3,2,1,0:T(8,128)S(1)}, u32[]{:S(2)}, u32[]{:S(2)}) collective-permute-start(f32[4,15,8,256]{3,2,1,0:T(8,128)S(1)} %get-tuple-element.62), channel_id=1, source_target_pairs={{0,16},{1,5},{2,18},{3,7},{4,20},{5,1},{6,22},{7,3},{8,24},{9,13},... | collective-permute-start | bytes 1474568 | tf_op jit(solution)/shard_map/ppermute | solution.py:446
  47.4 12.1 %collective-permute-start.4 = (f32[4,15,8,256]{3,2,1,0:T(8,128)S(1)}, f32[4,15,8,256]{3,2,1,0:T(8,128)S(1)}, u32[]{:S(2)}, u32[]{:S(2)}) collective-permute-start(f32[4,15,8,256]{3,2,1,0:T(8,128)S(1)} %get-tuple-element.62), channel_id=1, source_target_pairs={{0,8},{1,3},{2,10},{3,5},{4,12},{5,7},{6,14},{7,1},{8,16},{9,11},{... | collective-permute-start | bytes 1474568 | tf_op jit(solution)/shard_map/ppermute | solution.py:446
  47.8 11.8 %collective-permute-start.6 = (f32[4,15,8,256]{3,2,1,0:T(8,128)S(1)}, f32[4,15,8,256]{3,2,1,0:T(8,128)S(1)}, u32[]{:S(2)}, u32[]{:S(2)}) collective-permute-start(f32[4,15,8,256]{3,2,1,0:T(8,128)S(1)} %get-tuple-element.62), channel_id=1, source_target_pairs={{0,24},{1,7},{2,26},{3,1},{4,28},{5,3},{6,30},{7,5},{8,0},{9,15},{... | collective-permute-start | bytes 1474568 | tf_op jit(solution)/shard_map/ppermute | solution.py:446
  54.6 13.8 %copy-start.2 = (f32[2,2,2,8,2048]{4,3,2,1,0:T(8,128)}, f32[2,2,2,8,2048]{4,3,2,1,0:T(8,128)S(1)}, u32[]{:S(2)}) copy-start(f32[2,2,2,8,2048]{4,3,2,1,0:T(8,128)S(1)} %pad_maximum_fusion.3.cols_ref) | copy-start | bytes 1572868
  59.7 13.9 %copy-start.1 = (f32[4,4,15,8,256]{4,3,2,1,0:T(8,128)}, f32[4,4,15,8,256]{4,3,2,1,0:T(8,128)S(1)}, u32[]{:S(2)}) copy-start(f32[4,4,15,8,256]{4,3,2,1,0:T(8,128)S(1)} %pad_maximum_fusion.1.mine_ref) | copy-start | bytes 5898244
  59.7 13.9 %collective-permute-start.12 = (f32[4,4,15,8,256]{4,3,2,1,0:T(8,128)S(1)}, f32[4,4,15,8,256]{4,3,2,1,0:T(8,128)}, u32[]{:S(2)}, u32[]{:S(2)}) collective-permute-start(f32[4,4,15,8,256]{4,3,2,1,0:T(8,128)S(1)} %pad_maximum_fusion.1.mine_ref), channel_id=1, source_target_pairs={{0,1},{1,0},{2,3},{3,2},{4,5},{5,4},{6,7},{7,6},{8,9},{9,8},{10,11... | collective-permute-start | bytes 5898248 | tf_op jit(solution)/shard_map/ppermute | solution.py:458
  66.8 25.7 %collective-permute-start.10 = (f32[4,25,8,256]{3,2,1,0:T(8,128)S(1)}, f32[4,25,8,256]{3,2,1,0:T(8,128)}, u32[]{:S(2)}, u32[]{:S(2)}) collective-permute-start(f32[4,25,8,256]{3,2,1,0:T(8,128)S(1)} %pad_maximum_fusion.2), channel_id=1, source_target_pairs={{0,24},{1,7},{2,26},{3,1},{4,28},{5,3},{6,30},{7,5},{8,0},{9,15},{... | collective-permute-start | bytes 2457608 | tf_op jit(solution)/shard_map/ppermute | solution.py:446
  67.2 25.3 %collective-permute-start.9 = (f32[4,25,8,256]{3,2,1,0:T(8,128)S(1)}, f32[4,25,8,256]{3,2,1,0:T(8,128)}, u32[]{:S(2)}, u32[]{:S(2)}) collective-permute-start(f32[4,25,8,256]{3,2,1,0:T(8,128)S(1)} %pad_maximum_fusion.2), channel_id=1, source_target_pairs={{0,16},{1,5},{2,18},{3,7},{4,20},{5,1},{6,22},{7,3},{8,24},{9,13},... | collective-permute-start | bytes 2457608 | tf_op jit(solution)/shard_map/ppermute | solution.py:446
  67.5 24.9 %collective-permute-start.8 = (f32[4,25,8,256]{3,2,1,0:T(8,128)S(1)}, f32[4,25,8,256]{3,2,1,0:T(8,128)}, u32[]{:S(2)}, u32[]{:S(2)}) collective-permute-start(f32[4,25,8,256]{3,2,1,0:T(8,128)S(1)} %pad_maximum_fusion.2), channel_id=1, source_target_pairs={{0,8},{1,3},{2,10},{3,5},{4,12},{5,7},{6,14},{7,1},{8,16},{9,11},{... | collective-permute-start | bytes 2457608 | tf_op jit(solution)/shard_map/ppermute | solution.py:446
  68.3 24.1 %collective-permute-start.11 = (f32[2,2,2,8,2048]{4,3,2,1,0:T(8,128)S(1)}, f32[2,2,2,8,2048]{4,3,2,1,0:T(8,128)S(1)}, u32[]{:S(2)}, u32[]{:S(2)}) collective-permute-start(f32[2,2,2,8,2048]{4,3,2,1,0:T(8,128)S(1)} %pad_maximum_fusion.3.cols_ref), channel_id=1, source_target_pairs={{0,32},{32,0},{64,96},{96,64},{128,160},{160,128},{192,224},{224,1... | collective-permute-start | bytes 1572872 | tf_op jit(solution)/shard_map/ppermute | solution.py:462
  92.5 0.8 copy-start.8
  95.2 10.2 %copy-start = (f32[4,4,25,8,256]{4,3,2,1,0:T(8,128)}, f32[4,4,25,8,256]{4,3,2,1,0:T(8,128)S(1)}, u32[]{:S(2)}) copy-start(f32[4,4,25,8,256]{4,3,2,1,0:T(8,128)S(1)} %pad_maximum_fusion.mine_ref) | copy-start | bytes 9830404
  95.2 8.4 %collective-permute-start.13 = (f32[4,4,25,8,256]{4,3,2,1,0:T(8,128)S(1)}, f32[4,4,25,8,256]{4,3,2,1,0:T(8,128)S(1)}, u32[]{:S(2)}, u32[]{:S(2)}) collective-permute-start(f32[4,4,25,8,256]{4,3,2,1,0:T(8,128)S(1)} %pad_maximum_fusion.mine_ref), channel_id=1, source_target_pairs={{0,1},{1,0},{2,3},{3,2},{4,5},{5,4},{6,7},{7,6},{8,9},{9,8},{10,11... | collective-permute-start | bytes 9830408 | tf_op jit(solution)/shard_map/ppermute | solution.py:458
  103.7 1.7 %copy-start.7 = (f32[4,4,25,8,256]{4,3,2,1,0:T(8,128)}, f32[4,4,25,8,256]{4,3,2,1,0:T(8,128)S(1)}, u32[]{:S(2)}) copy-start(f32[4,4,25,8,256]{4,3,2,1,0:T(8,128)S(1)} %collective-permute-done.13.other_ref) | copy-start | bytes 9830404
